TPU v7x, 256 devices: a whole 4x4x8 slice. The times are simulated.
256 devices in a mesh: chan: 32 (over y, x, core), facet: 4 (over z_lo), vis: 2 (over z_hi).
Axes of the slice: x: 4, y: 4, z: 8 (z_hi: 2, z_lo: 4; z = z_hi * 4 + z_lo), core: 2. Of those that a mesh axis runs over, the one named last changes fastest.
Arguments:
- cube: float32 [32, 2048, 2048], P('chan', 'facet', 'vis'), may hold values from 0 to 1
- lowrank_dual: float32 [32, 2048, 2048], P('chan', 'facet', 'vis'), may hold values from -4 to 4
- vis_dual: float32 [32, 4, 2, 128, 128], P('chan', 'vis', None, 'facet'), may hold values from -3 to 3
- visibilities: float32 [32, 4, 2, 128, 128], P('chan', 'vis', None, 'facet'), may hold values from -3 to 3
- radii: float32 [32, 4], P('chan', 'vis'), may hold values from 32 to 128
- tiles: int32 [32, 4, 2], P('chan'), may hold values from 1 to 15
- facet_radius: float32 [4], P('facet'), may hold values from 512 to 4096
Outputs:
- cube_next: float32 [32, 2048, 2048], P('chan', 'facet', 'vis')
- lowrank_next: float32 [32, 2048, 2048], P('chan', 'facet', 'vis')
- vis_next: float32 [32, 4, 2, 128, 128], P('chan', 'vis', None, 'facet')
Inputs may be any that keep to these rules, and one draw needn't show every extreme that they name: `tiles`: row and column tile indices of blocks of 128 by 128 grid cells; blocks may repeat.
All inputs are finite; a program needn't handle non-finite values.
Results may differ from a plain program's by a relative error of at most 0.0003.
Values sent between devices are 32-bit elements; how exact they have to be, the bound alone decides.
A program may use at most 128 MiB of HBM per device.

v0:
```python
import math

import jax
import jax.numpy as jnp
from jax import lax
from jax.sharding import PartitionSpec as P

IMAGE = 2048
TILE = 128
NS_STEPS = 10
ITERS = 2


step_size = 0.5
highest = lax.Precision.HIGHEST


def make_tables(index_rows, positions):
    angle = index_rows[..., None] * positions % IMAGE
    theta = angle.astype(jnp.float32) * (2.0 * math.pi / IMAGE)
    scale = 1.0 / math.sqrt(IMAGE)
    return (jnp.cos(theta) * scale, jnp.sin(theta) * scale)


def block_tables(tile_index, rows, cols):
    offsets = jnp.arange(TILE, dtype=jnp.int32)
    freq_rows = tile_index[:, 0:1] * TILE + offsets[None, :]
    freq_cols = tile_index[:, 1:2] * TILE + offsets[None, :]
    cos_u, sin_u = make_tables(freq_rows, rows)
    cos_v, sin_v = make_tables(freq_cols, cols)
    return (cos_u, sin_u, cos_v, sin_v)


def forward_blocks(image, cos_u, sin_u, cos_v, sin_v):
    wreal = jnp.einsum("pq,bvq->bpv", image, cos_v, precision=highest)
    wimag = -jnp.einsum("pq,bvq->bpv", image, sin_v, precision=highest)
    real = jnp.einsum("bup,bpv->buv", cos_u, wreal, precision=highest) + jnp.einsum(
        "bup,bpv->buv", sin_u, wimag, precision=highest
    )
    imag = jnp.einsum("bup,bpv->buv", cos_u, wimag, precision=highest) - jnp.einsum(
        "bup,bpv->buv", sin_u, wreal, precision=highest
    )
    return jnp.stack([real, imag], axis=1)


def adjoint_blocks(dual, cos_u, sin_u, cos_v, sin_v):
    dreal = dual[:, 0]
    dimag = dual[:, 1]
    ereal = jnp.einsum("bup,buv->bpv", cos_u, dreal, precision=highest) - jnp.einsum(
        "bup,buv->bpv", sin_u, dimag, precision=highest
    )
    eimag = jnp.einsum("bup,buv->bpv", cos_u, dimag, precision=highest) + jnp.einsum(
        "bup,buv->bpv", sin_u, dreal, precision=highest
    )
    return jnp.einsum("bpv,bvq->pq", ereal, cos_v, precision=highest) - jnp.einsum(
        "bpv,bvq->pq", eimag, sin_v, precision=highest
    )


def inverse_root(gram, radius):
    count = gram.shape[0]
    eye = jnp.eye(count, dtype=jnp.float32)
    matrix = eye + gram / (radius * radius)
    trace = jnp.trace(matrix)
    current = matrix / trace
    inverse = eye
    for step in range(NS_STEPS):
        middle = 1.5 * eye - 0.5 * jnp.dot(
            inverse, current, precision=highest, preferred_element_type=jnp.float32
        )
        current = jnp.dot(current, middle, precision=highest, preferred_element_type=jnp.float32)
        inverse = jnp.dot(middle, inverse, precision=highest, preferred_element_type=jnp.float32)
    return inverse / jnp.sqrt(trace)


def on_device(cube, lowrank_dual, vis_dual, visibilities, radii, tiles, facet_radius):
    row_count = cube.shape[1]
    col_count = cube.shape[2]
    half_blocks = vis_dual.shape[1]
    quarter_rows = vis_dual.shape[3]
    facet_index = lax.axis_index("facet")
    column_index = lax.axis_index("vis")
    rows = facet_index * row_count + jnp.arange(row_count, dtype=jnp.int32)
    cols = column_index * col_count + jnp.arange(col_count, dtype=jnp.int32)
    tables = block_tables(tiles[0], rows, cols)
    radius = facet_radius[0]
    image_now = cube[0]
    lowrank = lowrank_dual
    dual_now = vis_dual[0]
    for step in range(ITERS):
        dual_rows = lax.all_gather(dual_now, "facet", axis=2, tiled=True)
        dual_full = lax.all_gather(dual_rows, "vis", axis=0, tiled=True)
        gradient = adjoint_blocks(dual_full, *tables)
        image_new = jnp.maximum(0.0, image_now - step_size * (lowrank[0] + gradient))
        extrap = 2.0 * image_new - image_now
        summed = lowrank + extrap[None]
        moved = lax.all_to_all(summed, "chan", split_axis=1, concat_axis=0, tiled=True)
        grouped = moved[:, None]
        partial_gram = jnp.einsum("lsrq,msrq->lm", grouped, grouped, precision=highest)
        gram = lax.psum(partial_gram, ("chan", "vis"))
        root = inverse_root(gram, radius)
        updated_group = jnp.einsum("lsrq,lm->msrq", grouped, root, precision=highest)
        lowrank = lax.all_to_all(
            updated_group[:, 0], "chan", split_axis=0, concat_axis=1, tiled=True
        )
        partial_value = forward_blocks(extrap, *tables)
        total = lax.psum(partial_value, ("facet", "vis"))
        owned = lax.dynamic_slice(
            total,
            (column_index * half_blocks, 0, facet_index * quarter_rows, 0),
            (half_blocks, 2, quarter_rows, total.shape[3]),
        )
        updated = dual_now + owned
        error = updated - visibilities[0]
        squares = jnp.sum(error * error, axis=(1, 2, 3))
        norms = jnp.sqrt(lax.psum(squares, "facet"))
        factor = radii[0] / jnp.maximum(norms, radii[0])
        dual_now = updated - (visibilities[0] + error * factor[:, None, None, None])
        image_now = image_new
    return (image_now[None], lowrank, dual_now[None])


def solution(mesh):
    placed = (
        P("chan", "facet", "vis"),
        P("chan", "facet", "vis"),
        P("chan", "vis", None, "facet", None),
        P("chan", "vis", None, "facet", None),
        P("chan", "vis"),
        P("chan", None, None),
        P("facet"),
    )
    return jax.shard_map(
        on_device,
        mesh=mesh,
        in_specs=placed,
        out_specs=(
            P("chan", "facet", "vis"),
            P("chan", "facet", "vis"),
            P("chan", "vis", None, "facet", None),
        ),
        check_vma=False,
    )
```

profile of v0, /device:TPU:8, one launch (start us, length us, event | category | flops | bytes accessed | tf_op | source)
XLA Modules:
  0.0 1316.2 jit_solution(4187696355042154657)
XLA Ops:
  7.9 15.2 %all-gather = f32[1,2,2,128,128]{4,3,2,0,1:T(8,128)S(1)} all-gather(f32[1,2,2,32,128]{4,3,2,0,1:T(8,128)} %bitcast.261), channel_id=2, replica_groups=mesh['chan'=32,'facet'=4,'vis'=2] {'facet'}, dimensions={3}, use_global_device_ids=true | all-gather | bytes 327680 | tf_op jit(solution)/shard_map/all_gather | solution.py:91
  23.1 13.1 all-gather.1
  47.6 6.0 convolution_add_fusion.1
  59.2 11.3 fusion.34
  70.5 13.3 %bitcast_add_fusion.1 = (f32[1,512,1024]{2,1,0:T(8,128)S(1)}, f32[512,1024]{1,0:T(8,128)}) fusion(f32[1,512,1024]{2,1,0:T(8,128)S(1)} %copy-done.2, f32[1,512,1024]{2,1,0:T(8,128)S(1)} %copy-done.3, f32[4,512,128]{2,1,0:T(8,128)S(1)} %convolution_add_fusion.1, s32[1024]{0:T(1024)S(1)} %iota_add_fusion, s32[4,128]{1,0:T(4,128)S(1)} %get-tuple-element.21, ...), kind=kOutput, calls=%fused_computation.22 | convolution fusion | flops 3233284096 | bytes 11540480 | tf_op jit(solution)/shard_map/bpv,bvq->pq/dot_general | solution.py:55
  87.5 7.6 all-to-all-start
  95.2 13.0 fusion.27
  113.5 11.5 fusion.13
  142.0 75.1 %all-reduce.3.cloned.1.call-done = f32[4,2,128,128]{3,2,0,1:T(8,128)} async-done(((f32[4,2,128,128]{3,2,0,1:T(8,128)}), f32[4,2,128,128]{3,2,0,1:T(8,128)}) %all-reduce.3.cloned.1.call-update) | async-done | bytes 524304 | tf_op jit(solution)/shard_map/psum | solution.py:107
  218.0 11.1 psum.44
  234.0 372.4 %psum.42 = f32[32,32]{1,0:T(8,128)S(1)} all-reduce(f32[32,32]{1,0:T(8,128)S(1)} %fusion.39), channel_id=1, replica_groups=mesh['chan'=32,'facet'=4,'vis'=2] {'chan','vis'}, use_global_device_ids=true, to_apply=%region_0.1 | all-reduce | flops 1024 | bytes 8192 | tf_op jit(solution)/shard_map/psum | solution.py:100
  618.9 36.1 %all-to-all-start.1 = ((f32[32,16,1024]{2,1,0:T(8,128)}), f32[32,16,1024]{2,1,0:T(8,128)S(1)}, u32[]{:S(2)}, u32[]{:S(2)}) async-start(f32[32,16,1024]{2,1,0:T(8,128)} %copy.61), calls=%async_computation.1 | async-start | bytes 4194304 | tf_op jit(solution)/shard_map/all_to_all | solution.py:103
  656.0 14.4 %all_gather.14 = f32[2,2,128,128]{3,2,0,1:T(8,128)S(1)} all-gather(f32[2,2,32,128]{3,2,0,1:T(8,128)S(1)} %fusion.94), channel_id=1, replica_groups=mesh['chan'=32,'facet'=4,'vis'=2] {'facet'}, dimensions={2}, use_global_device_ids=true | all-gather | bytes 327680 | tf_op jit(solution)/shard_map/all_gather | solution.py:91
  670.4 14.3 %all_gather.15 = f32[4,2,128,128]{3,2,0,1:T(8,128)S(1)} all-gather(f32[2,2,128,128]{3,2,0,1:T(8,128)S(1)} %all_gather.14), channel_id=1, replica_groups=mesh['chan'=32,'facet'=4,'vis'=2] {'vis'}, dimensions={0}, use_global_device_ids=true | all-gather | bytes 786432 | tf_op jit(solution)/shard_map/all_gather | solution.py:92
  696.0 5.9 convolution_add_fusion
  707.5 12.9 fusion.33
  720.4 15.6 %bitcast_add_fusion = (f32[512,1024]{1,0:T(8,128)S(1)}, f32[512,1024]{1,0:T(8,128)}) fusion(f32[32,16,1024]{2,1,0:T(8,128)S(1)} %all-to-all-done.1, f32[512,1024]{1,0:T(8,128)} %get-tuple-element.18, f32[4,512,128]{2,1,0:T(8,128)S(1)} %convolution_add_fusion, s32[1024]{0:T(1024)S(1)} %iota_add_fusion, s32[4,128]{1,0:T(4,128)S(1)} %get-tuple-element.21, ...), kind=kOutput, calls=%fused_computation.21 | convolution fusion | flops 3233284096 | bytes 11540480 | tf_op jit(solution)/shard_map/bpv,bvq->pq/dot_general | solution.py:55
  739.4 7.8 all-to-all-start.2
  747.3 13.0 fusion.5
  760.3 12.8 fusion.30
  778.7 372.8 %psum.45 = f32[32,32]{1,0:T(8,128)S(1)} all-reduce(f32[32,32]{1,0:T(8,128)S(1)} %fusion.42), channel_id=1, replica_groups=mesh['chan'=32,'facet'=4,'vis'=2] {'chan','vis'}, use_global_device_ids=true, to_apply=%region_5.6 | all-reduce | flops 1024 | bytes 8192 | tf_op jit(solution)/shard_map/psum | solution.py:100
  1164.0 35.9 %all-to-all-start.3 = ((f32[32,16,1024]{2,1,0:T(8,128)}), f32[32,16,1024]{2,1,0:T(8,128)S(1)}, u32[]{:S(2)}, u32[]{:S(2)}) async-start(f32[32,16,1024]{2,1,0:T(8,128)} %copy.73), calls=%async_computation.3 | async-start | bytes 4194304 | tf_op jit(solution)/shard_map/all_to_all | solution.py:103
  1221.4 72.6 %all-reduce.5.cloned.1.call-done = f32[4,2,128,128]{3,2,0,1:T(8,128)} async-done(((f32[4,2,128,128]{3,2,0,1:T(8,128)}), f32[4,2,128,128]{3,2,0,1:T(8,128)}) %all-reduce.5.cloned.1.call-update) | async-done | bytes 524304 | tf_op jit(solution)/shard_map/psum | solution.py:107
  1295.0 11.1 psum.47
  (125 shorter events, 124.4 us)
Async XLA Ops:
  59.2 11.3 copy-start.2
  59.2 11.3 copy-start.3
  87.5 141.6 %all-to-all-start = ((f32[1,512,1024]{2,0,1:T(1,128)}), f32[1,512,1024]{2,0,1:T(1,128)}, u32[]{:S(2)}, u32[]{:S(2)}) async-start(f32[1,512,1024]{2,0,1:T(1,128)} %copy.56), calls=%async_computation | async-start | bytes 4194304 | tf_op jit(solution)/shard_map/all_to_all | solution.py:97
  95.1 122.0 %all-reduce.3.cloned.1.call-start = ((), (), s32[]{:S(2)}) async-start(), calls=%async_computation.4 | async-start | bytes 1048576 | tf_op jit(solution)/shard_map/psum | solution.py:107
  108.1 5.4 copy-start.6
  135.5 81.6 %copy-start = (f32[1,2,2,32,128]{4,3,2,1,0:T(8,128)S(1)}, f32[1,2,2,32,128]{4,3,2,1,0:T(8,128)}, u32[]{:S(2)}) copy-start(f32[1,2,2,32,128]{4,3,2,1,0:T(8,128)} %param.10) | copy-start | bytes 196612
  135.5 81.6 %copy-start.1 = (f32[1,2,2,32,128]{4,3,2,1,0:T(8,128)S(1)}, f32[1,2,2,32,128]{4,3,2,1,0:T(8,128)}, u32[]{:S(2)}) copy-start(f32[1,2,2,32,128]{4,3,2,1,0:T(8,128)} %param.9) | copy-start | bytes 196612
  618.9 36.1 %copy-start.4 = (f32[1,2]{1,0:T(1,128)S(1)}, f32[1,2]{1,0:T(1,128)}, u32[]{:S(2)}) copy-start(f32[1,2]{1,0:T(1,128)} %param.11) | copy-start | bytes 28
  618.9 101.4 %all-to-all-start.1 = ((f32[32,16,1024]{2,1,0:T(8,128)}), f32[32,16,1024]{2,1,0:T(8,128)S(1)}, u32[]{:S(2)}, u32[]{:S(2)}) async-start(f32[32,16,1024]{2,1,0:T(8,128)} %copy.61), calls=%async_computation.1 | async-start | bytes 4194304 | tf_op jit(solution)/shard_map/all_to_all | solution.py:103
  739.4 7.9 copy-start.5
  739.4 34.2 %all-to-all-start.2 = ((f32[1,512,1024]{2,0,1:T(1,128)}), f32[1,512,1024]{2,0,1:T(1,128)}, u32[]{:S(2)}, u32[]{:S(2)}) async-start(f32[1,512,1024]{2,0,1:T(1,128)} %copy.68), calls=%async_computation.2 | async-start | bytes 4194304 | tf_op jit(solution)/shard_map/all_to_all | solution.py:97
  747.3 13.1 copy-start.7
  1164.0 143.6 %all-to-all-start.3 = ((f32[32,16,1024]{2,1,0:T(8,128)}), f32[32,16,1024]{2,1,0:T(8,128)S(1)}, u32[]{:S(2)}, u32[]{:S(2)}) async-start(f32[32,16,1024]{2,1,0:T(8,128)} %copy.73), calls=%async_computation.3 | async-start | bytes 4194304 | tf_op jit(solution)/shard_map/all_to_all | solution.py:103
  1200.0 94.1 %all-reduce.5.cloned.1.call-start = ((), (), s32[]{:S(2)}) async-start(), calls=%async_computation.5 | async-start | bytes 1048576 | tf_op jit(solution)/shard_map/psum | solution.py:107
  1200.2 5.0 copy-start.8
Sparse Core Ops, SparseCore 0:
  141.5 75.5 all-reduce.2
  1221.5 72.4 all-reduce.4
where the time goes:
time: 1330 us; the launch traced here: 1320 us
  blocking collectives  824 us (62%)
  matrix products  213 us (16%)
  waiting for transfers between devices  148 us (11%)
  starting transfers between devices  87.8 us (7%)
  local copies, waits for them, and re-layouts  18.3 us (1%)
  between operations  17.1 us (1%)
    psum x2, blocking collectives, on_device(): gram = lax.psum(partial_gram, ('chan', 'vis'))  745 us
    psum x2, waiting for transfers between devices, on_device(): total = lax.psum(partial_value, ('facet', 'vis'))  148 us
    all_to_all x2, starting transfers between devices, on_device(): lax.all_to_all(updated_group[:, 0], 'chan', split_axis=0, concat_axis=1,...  72 us
    all_gather x2, blocking collectives, on_device(): dual_rows = lax.all_gather(dual_now, 'facet', axis=2, tiled=True)  29.6 us
    dot_general x2, matrix products, adjoint_blocks(): jnp.einsum('bpv,bvq->pq', eimag, sin_v, precision=highest)  28.9 us
    all_gather x2, blocking collectives, on_device(): dual_full = lax.all_gather(dual_rows, 'vis', axis=0, tiled=True)  27.5 us
  transfers between devices with their start and end apart: 6, of which 3 were waited for; matrix products, arithmetic and copies ran while one was open for 10% of the time, Pallas kernels for 0%

commit v1 on v0

--- a/solution.py
+++ b/solution.py
@@ -1,14 +1,19 @@
+import functools
 import math
 
 import jax
 import jax.numpy as jnp
 from jax import lax
+from jax.experimental import pallas as pl
+from jax.experimental.pallas import tpu as pltpu
 from jax.sharding import PartitionSpec as P
 
 IMAGE = 2048
 TILE = 128
 NS_STEPS = 10
 ITERS = 2
+CHANNELS = 32
+PITCH = 136
 
 
 step_size = 0.5
@@ -57,20 +62,194 @@
     )
 
 
+def chan_peer(offset):
+    me = lax.axis_index("chan")
+    dy, dx, dc = offset
+    y = lax.rem(me // 8 + dy, 4)
+    x = lax.rem(me // 2 + dx, 4)
+    return (y * 4 + x) * 2 + lax.rem(me + dc, 2)
+
+
+def hops(offset):
+    return min(offset[0], 4 - offset[0]) + min(offset[1], 4 - offset[1])
+
+
+OFFSETS = sorted(
+    [(dy, dx, dc) for dy in range(4) for dx in range(4) for dc in range(2) if (dy, dx, dc) != (0, 0, 0)],
+    key=lambda offset: -hops(offset),
+)
+GROUP_A = [(0, dx, dc) for dx in (2, 1, 3, 0) for dc in range(2) if (dx, dc) != (0, 0)]
+GROUP_B = [(dy, dv) for dv in (1, 0) for dy in (2, 1, 3, 0) if (dy, dv) != (0, 0)]
+
+
+def group_b_device(offset):
+    me = lax.axis_index("chan")
+    return {
+        "chan": lax.rem(me // 8 + offset[0], 4) * 8 + lax.rem(me, 8),
+        "vis": lax.rem(lax.axis_index("vis") + offset[1], 2),
+    }
+
+
+def remote(source, target, send_sem, recv_sem, device):
+    return pltpu.make_async_remote_copy(
+        src_ref=source,
+        dst_ref=target,
+        send_sem=send_sem,
+        recv_sem=recv_sem,
+        device_id=device,
+        device_id_type=pl.DeviceIdType.MESH,
+    )
+
+
+def split_bf16(value):
+    high = value.astype(jnp.bfloat16)
+    return high, (value - high.astype(jnp.float32)).astype(jnp.bfloat16)
+
+
+def entry_barrier():
+    barrier = pltpu.get_barrier_semaphore()
+    peers = [{"chan": chan_peer(offset)} for offset in OFFSETS]
+    peers += [group_b_device(offset) for offset in GROUP_B if offset[1]]
+    for device in peers:
+        pl.semaphore_signal(barrier, inc=1, device_id=device, device_id_type=pl.DeviceIdType.MESH)
+    pl.semaphore_wait(barrier, len(peers))
+
+
+def exchange(source, target, sends, recvs):
+    copies = []
+    for n, offset in enumerate(OFFSETS):
+        j = chan_peer(offset)
+        copies.append(remote(source(j), target, sends.at[n], recvs.at[n], {"chan": j}))
+        copies[-1].start()
+    return copies
+
+
+def sum_group(value, send_buf, recv_buf, sends, recvs, devices):
+    send_buf[...] = value
+    copies = []
+    for n, device in enumerate(devices):
+        copies.append(remote(send_buf, recv_buf.at[n], sends.at[n], recvs.at[n], device))
+        copies[-1].start()
+    for copy in copies:
+        copy.wait()
+    for n in range(len(devices)):
+        value = value + recv_buf[n]
+    return value
+
+
+def stripes(group):
+    return [pl.ds(group * 8 + s, CHANNELS, stride=PITCH) for s in range(8)]
+
+
+def gram_of(received, halves):
+    def body(group, total):
+        block = jnp.concatenate([received[rows, :] for rows in stripes(group)], axis=1)
+        both = jnp.concatenate(split_bf16(block), axis=0)
+        halves[group] = both
+        return total + lax.dot_general(
+            both, both, (((1,), (1,)), ((), ())), preferred_element_type=jnp.float32
+        )
+
+    total = lax.fori_loop(0, TILE // 8, body, jnp.zeros((2 * CHANNELS, 2 * CHANNELS), jnp.float32))
+    total = total[:CHANNELS] + total[CHANNELS:]
+    return total[:, :CHANNELS] + total[:, CHANNELS:]
+
+
+def mix_into(target, halves, root):
+    high, low = split_bf16(root)
+    weights = jnp.concatenate(
+        [jnp.concatenate([high, high], axis=1), jnp.concatenate([low, low], axis=1)], axis=0
+    )
+
+    def body(group, carry):
+        mixed = jnp.dot(weights, halves[group], preferred_element_type=jnp.float32)
+        mixed = mixed[:CHANNELS] + mixed[CHANNELS:]
+        for s, rows in enumerate(stripes(group)):
+            target[rows, :] = mixed[:, s * 128 : (s + 1) * 128]
+        return carry
+
+    lax.fori_loop(0, TILE // 8, body, 0)
+
+
+def matmul(a, b):
+    return jnp.dot(a, b, precision=highest, preferred_element_type=jnp.float32)
+
+
 def inverse_root(gram, radius):
-    count = gram.shape[0]
-    eye = jnp.eye(count, dtype=jnp.float32)
+    rows = lax.broadcasted_iota(jnp.int32, gram.shape, 0)
+    eye = jnp.where(rows == lax.broadcasted_iota(jnp.int32, gram.shape, 1), 1.0, 0.0)
     matrix = eye + gram / (radius * radius)
-    trace = jnp.trace(matrix)
+    trace = jnp.sum(matrix * eye, axis=(0, 1), keepdims=True)
     current = matrix / trace
     inverse = eye
     for step in range(NS_STEPS):
-        middle = 1.5 * eye - 0.5 * jnp.dot(
-            inverse, current, precision=highest, preferred_element_type=jnp.float32
-        )
-        current = jnp.dot(current, middle, precision=highest, preferred_element_type=jnp.float32)
-        inverse = jnp.dot(middle, inverse, precision=highest, preferred_element_type=jnp.float32)
+        product = matmul(inverse, current) if step else current
+        middle = 1.5 * eye - 0.5 * product
+        inverse = matmul(middle, inverse) if step else middle
+        if step < NS_STEPS - 1:
+            current = matmul(current, middle)
     return inverse / jnp.sqrt(trace)
+
+
+def pack(gram):
+    return jnp.concatenate([gram[8 * k : 8 * k + 8] for k in range(4)], axis=1)
+
+
+def unpack(packed):
+    return jnp.concatenate([packed[:, 32 * k : 32 * k + 32] for k in range(4)], axis=0)
+
+
+def lane_rows(index):
+    return pl.ds(pl.multiple_of(index * PITCH, 8), TILE)
+
+
+def lowrank_kernel(z_ref, radius_ref, p_ref, received, mixed, halves, sums, parts, sends, recvs, small_sends, small_recvs):
+    me = lax.axis_index("chan")
+    entry_barrier()
+    received[lane_rows(me), :] = z_ref[me]
+    copies = exchange(lambda j: z_ref.at[j], received.at[lane_rows(me), :], sends.at[0], recvs.at[0])
+    for copy in copies:
+        copy.wait()
+    total = pack(gram_of(received, halves))
+    total = sum_group(
+        total, sums.at[0], parts.at[0], small_sends.at[0], small_recvs.at[0],
+        [{"chan": chan_peer(offset)} for offset in GROUP_A],
+    )
+    total = sum_group(
+        total, sums.at[1], parts.at[1], small_sends.at[1], small_recvs.at[1],
+        [group_b_device(offset) for offset in GROUP_B],
+    )
+    root = inverse_root(unpack(total), radius_ref[0])
+    mix_into(mixed, halves, root)
+    p_ref[me] = mixed[lane_rows(me), :]
+    copies = exchange(lambda j: mixed.at[lane_rows(j), :], p_ref.at[me], sends.at[1], recvs.at[1])
+    for copy in copies:
+        copy.wait()
+
+
+def lowrank_step(tiles, radius, number):
+    dma = pltpu.SemaphoreType.DMA
+    return pl.pallas_call(
+        lowrank_kernel,
+        out_shape=jax.ShapeDtypeStruct((CHANNELS, TILE, TILE), jnp.float32),
+        in_specs=[pl.BlockSpec(memory_space=pltpu.VMEM), pl.BlockSpec(memory_space=pltpu.SMEM)],
+        out_specs=pl.BlockSpec(memory_space=pltpu.VMEM),
+        scratch_shapes=[
+            pltpu.VMEM((CHANNELS * PITCH, TILE), jnp.float32),
+            pltpu.VMEM((CHANNELS * PITCH, TILE), jnp.float32),
+            pltpu.VMEM((TILE // 8, 2 * CHANNELS, 1024), jnp.bfloat16),
+            pltpu.VMEM((2, 8, 128), jnp.float32),
+            pltpu.VMEM((2, 7, 8, 128), jnp.float32),
+            dma((2, 31)),
+            dma((2, 31)),
+            dma((2, 7)),
+            dma((2, 7)),
+        ],
+        compiler_params=pltpu.CompilerParams(
+            collective_id=number, has_side_effects=True, vmem_limit_bytes=40 << 20
+        ),
+        name="lowrank",
+    )(tiles, radius)
 
 
 def on_device(cube, lowrank_dual, vis_dual, visibilities, radii, tiles, facet_radius):
@@ -83,7 +262,6 @@
     rows = facet_index * row_count + jnp.arange(row_count, dtype=jnp.int32)
     cols = column_index * col_count + jnp.arange(col_count, dtype=jnp.int32)
     tables = block_tables(tiles[0], rows, cols)
-    radius = facet_radius[0]
     image_now = cube[0]
     lowrank = lowrank_dual
     dual_now = vis_dual[0]
@@ -94,15 +272,9 @@
         image_new = jnp.maximum(0.0, image_now - step_size * (lowrank[0] + gradient))
         extrap = 2.0 * image_new - image_now
         summed = lowrank + extrap[None]
-        moved = lax.all_to_all(summed, "chan", split_axis=1, concat_axis=0, tiled=True)
-        grouped = moved[:, None]
-        partial_gram = jnp.einsum("lsrq,msrq->lm", grouped, grouped, precision=highest)
-        gram = lax.psum(partial_gram, ("chan", "vis"))
-        root = inverse_root(gram, radius)
-        updated_group = jnp.einsum("lsrq,lm->msrq", grouped, root, precision=highest)
-        lowrank = lax.all_to_all(
-            updated_group[:, 0], "chan", split_axis=0, concat_axis=1, tiled=True
-        )
+        pieces = summed[0].reshape(4, TILE, 8, TILE).transpose(0, 2, 1, 3)
+        pieces = lowrank_step(pieces.reshape(CHANNELS, TILE, TILE), facet_radius, 0)
+        lowrank = pieces.reshape(4, 8, TILE, TILE).transpose(0, 2, 1, 3).reshape(summed.shape)
         partial_value = forward_blocks(extrap, *tables)
         total = lax.psum(partial_value, ("facet", "vis"))
         owned = lax.dynamic_slice(

time: 1330 us -> 455 us (0.34)
  blocking collectives: 824 us -> 76.8 us
  Pallas kernels: 0 us -> 153 us
  waiting for transfers between devices: 148 us -> 0.06 us
  starting transfers between devices: 87.8 us -> 0.08 us
  matrix products: 213 us -> 179 us
    psum x2 -> x0, blocking collectives: 745 us -> none  [on_device(): gram = lax.psum(partial_gram, ('chan', 'vis'))]
    pallas_call x0 -> x2, Pallas kernels: none -> 153 us  [lowrank_step(): pl.pallas_call(lowrank_kernel, out_shape=jax.ShapeDtypeStruct((CHANNELS,...]
    psum x2, waiting for transfers between devices: 148 us -> 0.02 us  [on_device(): total = lax.psum(partial_value, ('facet', 'vis'))]
    all_to_all x4 -> x0, starting transfers between devices: 87.5 us -> none  [the longest x2 72 us: on_device(): lax.all_to_all(updated_group[:, 0], 'chan', split_axis=0, concat_axis=1,...]
    dot_general x62 -> x0, matrix products: 23 us -> none  [the longest x2 6.03 us: on_device(): jnp.einsum('lsrq,lm->msrq', grouped, root, precision=highest)]
  transfers between devices with their start and end apart: 6 -> 2, of which waited for: 3 -> 0; matrix products, arithmetic and copies ran while one was open for 10% -> 2% of each run, Pallas kernels for 0% -> 34%
where the time goes in v1:
time: 455 us; the launch traced here: 446 us
  matrix products  179 us (39%)
  Pallas kernels  153 us (34%)
  blocking collectives  76.8 us (17%)
  between operations  15.5 us (3%)
  other arithmetic  12.5 us (3%)
  local copies, waits for them, and re-layouts  9.19 us (2%)
    pallas_call x2, Pallas kernels, lowrank_step(): pl.pallas_call(lowrank_kernel, out_shape=jax.ShapeDtypeStruct((CHANNELS,...  153 us
    all_gather x2, blocking collectives, on_device(): dual_rows = lax.all_gather(dual_now, 'facet', axis=2, tiled=True)  29.7 us
    all_gather x2, blocking collectives, on_device(): dual_full = lax.all_gather(dual_rows, 'vis', axis=0, tiled=True)  25.5 us
    dot_general x2, matrix products, adjoint_blocks(): jnp.einsum('bpv,bvq->pq', eimag, sin_v, precision=highest)  23.8 us
    dot_general x2, matrix products, forward_blocks(): wreal = jnp.einsum('pq,bvq->bpv', image, cos_v, precision=highest)  23.2 us
    dot_general x2, matrix products, forward_blocks(): wimag = -jnp.einsum('pq,bvq->bpv', image, sin_v, precision=highest)  23.1 us
    dot_general x2, matrix products, adjoint_blocks(): jnp.einsum('bpv,bvq->pq', ereal, cos_v, precision=highest)  22.7 us
    psum x2, blocking collectives, on_device(): norms = jnp.sqrt(lax.psum(squares, 'facet'))  21.6 us
  transfers between devices with their start and end apart: 2, of which 0 were waited for; matrix products, arithmetic and copies ran while one was open for 2% of the time, Pallas kernels for 34%

profile of v1, /device:TPU:8, one launch (start us, length us, event | category | flops | bytes accessed | tf_op | source)
XLA Modules:
  0.0 445.8 jit_solution(6051575452723292808)
XLA Ops:
  8.0 15.2 %all-gather = f32[1,2,2,128,128]{4,3,2,0,1:T(8,128)S(1)} all-gather(f32[1,2,2,32,128]{4,3,2,0,1:T(8,128)} %bitcast.168), channel_id=2, replica_groups=mesh['chan'=32,'facet'=4,'vis'=2] {'facet'}, dimensions={3}, use_global_device_ids=true | all-gather | bytes 327680 | tf_op jit(solution)/shard_map/all_gather | solution.py:269
  23.2 13.1 %all-gather.1 = f32[1,4,2,128,128]{4,3,2,0,1:T(8,128)S(1)} all-gather(f32[1,2,2,128,128]{4,3,2,0,1:T(8,128)S(1)} %all-gather), channel_id=3, replica_groups=mesh['chan'=32,'facet'=4,'vis'=2] {'vis'}, dimensions={1}, use_global_device_ids=true | all-gather | bytes 786432 | tf_op jit(solution)/shard_map/all_gather | solution.py:270
  36.4 5.6 %fusion.58 = f32[4,512,128]{2,1,0:T(8,128)S(1)} fusion(s32[512]{0:T(512)S(1)} %iota_add_fusion.2, s32[4,128]{1,0:T(4,128)S(1)} %get-tuple-element.12, f32[4,2,128,128]{3,2,1,0:T(8,128)S(1)} %bitcast.169), kind=kOutput, calls=%fused_computation.77 | convolution fusion | flops 406585344 | bytes 1314816 | tf_op jit(solution)/shard_map/bup,buv->bpv/dot_general | solution.py:54
  42.0 5.6 %fusion.57 = f32[4,512,128]{2,1,0:T(8,128)S(1)} fusion(s32[512]{0:T(512)S(1)} %iota_add_fusion.2, s32[4,128]{1,0:T(4,128)S(1)} %get-tuple-element.12, f32[4,2,128,128]{3,2,1,0:T(8,128)S(1)} %bitcast.170), kind=kOutput, calls=%fused_computation.76 | convolution fusion | flops 406585344 | bytes 1314816 | tf_op jit(solution)/shard_map/bup,buv->bpv/dot_general | solution.py:57
  47.6 5.8 %convolution_subtract_fusion.1 = f32[4,512,128]{2,1,0:T(8,128)S(1)} fusion(f32[4,512,128]{2,1,0:T(8,128)S(1)} %fusion.58, s32[512]{0:T(512)S(1)} %iota_add_fusion.2, s32[4,128]{1,0:T(4,128)S(1)} %get-tuple-element.12, f32[4,2,128,128]{3,2,1,0:T(8,128)S(1)} %bitcast.171), kind=kOutput, calls=%fused_computation.44 | convolution fusion | flops 406847488 | bytes 2363392 | tf_op jit(solution)/shard_map/bup,buv->bpv/dot_general | solution.py:54
  53.4 5.6 %convolution_add_fusion.1 = f32[4,512,128]{2,1,0:T(8,128)S(1)} fusion(f32[4,512,128]{2,1,0:T(8,128)S(1)} %fusion.57, s32[512]{0:T(512)S(1)} %iota_add_fusion.2, s32[4,128]{1,0:T(4,128)S(1)} %get-tuple-element.12, f32[4,2,128,128]{3,2,1,0:T(8,128)S(1)} %bitcast.172), kind=kOutput, calls=%fused_computation.43 | convolution fusion | flops 406847488 | bytes 2363392 | tf_op jit(solution)/shard_map/bup,buv->bpv/dot_general | solution.py:57
  59.0 11.4 %fusion.27 = f32[512,1024,1]{1,0,2:T(8,128)S(1)} fusion(f32[4,512,128]{2,1,0:T(8,128)S(1)} %convolution_subtract_fusion.1, s32[1024]{0:T(1024)S(1)} %iota_add_fusion, s32[4,128]{1,0:T(4,128)S(1)} %get-tuple-element.11), kind=kOutput, calls=%fused_computation.46 | convolution fusion | flops 3229089792 | bytes 3151872 | tf_op jit(solution)/shard_map/bpv,bvq->pq/dot_general | solution.py:60
  70.4 11.9 %fusion.19 = f32[512,1024]{1,0:T(8,128)S(1)} fusion(f32[512,1024,1]{1,0,2:T(8,128)S(1)} %fusion.27, f32[1,512,1024]{2,1,0:T(8,128)S(1)} %copy-done.3, f32[1,512,1024]{2,1,0:T(8,128)S(1)} %copy-done.4, f32[4,512,128]{2,1,0:T(8,128)S(1)} %convolution_add_fusion.1, s32[1024]{0:T(1024)S(1)} %iota_add_fusion, s32[4,128]{1,0:T(4,128)S(1)} %get-tuple-element.11), kind=kOutput, calls=%fused_computation.29 | convolution fusion | flops 3231711232 | bytes 9443328 | tf_op jit(solution)/shard_map/bpv,bvq->pq/dot_general | solution.py:60
  82.3 11.5 %fusion.13 = f32[4,128,512]{2,1,0:T(8,128)S(1)} fusion(s32[1024]{0:T(1024)S(1)} %iota_add_fusion, s32[4,128]{1,0:T(4,128)S(1)} %get-tuple-element.11, f32[1,512,1024]{2,1,0:T(8,128)S(1)} %copy-done.4, f32[512,1024]{1,0:T(8,128)S(1)} %fusion.19), kind=kOutput, calls=%fused_computation.21 | convolution fusion | flops 3230138368 | bytes 5249024 | tf_op jit(solution)/shard_map/pq,bvq->bpv/dot_general | solution.py:40
  93.8 11.6 %fusion.20 = f32[4,128,512]{2,1,0:T(8,128)S(1)} fusion(s32[1024]{0:T(1024)S(1)} %iota_add_fusion, s32[4,128]{1,0:T(4,128)S(1)} %get-tuple-element.11, f32[1,512,1024]{2,1,0:T(8,128)S(1)} %copy-done.4, f32[512,1024]{1,0:T(8,128)S(1)} %fusion.19), kind=kOutput, calls=%fused_computation.39 | convolution fusion | flops 3230400512 | bytes 5249024 | tf_op jit(solution)/shard_map/pq,bvq->bpv/dot_general | solution.py:41
  131.4 79.9 %lowrank.2 = f32[32,128,128]{2,1,0:T(8,128)S(1)} custom-call(f32[32,128,128]{2,1,0:T(8,128)S(1)} %bitcast.159, f32[1]{0:T(128)S(6)} %copy.49.radius_ref), custom_call_target="tpu_custom_call" | custom-call | tf_op jit(solution)/shard_map/lowrank/pallas_call | solution.py:232
  216.4 10.5 %psum.29 = f32[2]{0:T(128)S(1)} all-reduce(f32[2]{0:T(128)S(1)} %multiply_reduce_fusion.1), channel_id=1, replica_groups=mesh['chan'=32,'facet'=4,'vis'=2] {'facet'}, use_global_device_ids=true, to_apply=%region_2.3 | all-reduce | flops 2 | bytes 16 | tf_op jit(solution)/shard_map/psum | solution.py:288
  227.8 14.5 %all_gather.14 = f32[2,2,128,128]{3,2,0,1:T(8,128)S(1)} all-gather(f32[2,2,32,128]{3,2,0,1:T(8,128)S(1)} %fusion.59), channel_id=1, replica_groups=mesh['chan'=32,'facet'=4,'vis'=2] {'facet'}, dimensions={2}, use_global_device_ids=true | all-gather | bytes 327680 | tf_op jit(solution)/shard_map/all_gather | solution.py:269
  242.3 12.4 %all_gather.15 = f32[4,2,128,128]{3,2,0,1:T(8,128)S(1)} all-gather(f32[2,2,128,128]{3,2,0,1:T(8,128)S(1)} %all_gather.14), channel_id=1, replica_groups=mesh['chan'=32,'facet'=4,'vis'=2] {'vis'}, dimensions={0}, use_global_device_ids=true | all-gather | bytes 786432 | tf_op jit(solution)/shard_map/all_gather | solution.py:270
  254.7 5.6 %fusion.53 = f32[4,512,128]{2,1,0:T(8,128)S(1)} fusion(s32[512]{0:T(512)S(1)} %iota_add_fusion.2, s32[4,128]{1,0:T(4,128)S(1)} %get-tuple-element.12, f32[4,2,128,128]{3,2,0,1:T(8,128)S(1)} %all_gather.15), kind=kOutput, calls=%fused_computation.72 | convolution fusion | flops 406585344 | bytes 1314816 | tf_op jit(solution)/shard_map/bup,buv->bpv/dot_general | solution.py:57
  260.3 5.6 %fusion.54 = f32[4,512,128]{2,1,0:T(8,128)S(1)} fusion(s32[512]{0:T(512)S(1)} %iota_add_fusion.2, s32[4,128]{1,0:T(4,128)S(1)} %get-tuple-element.12, f32[4,2,128,128]{3,2,0,1:T(8,128)S(1)} %all_gather.15), kind=kOutput, calls=%fused_computation.73 | convolution fusion | flops 406585344 | bytes 1314816 | tf_op jit(solution)/shard_map/bup,buv->bpv/dot_general | solution.py:54
  265.8 6.0 %convolution_add_fusion = f32[4,512,128]{2,1,0:T(8,128)S(1)} fusion(f32[4,512,128]{2,1,0:T(8,128)S(1)} %fusion.53, s32[512]{0:T(512)S(1)} %iota_add_fusion.2, s32[4,128]{1,0:T(4,128)S(1)} %get-tuple-element.12, f32[4,2,128,128]{3,2,0,1:T(8,128)S(1)} %all_gather.15), kind=kOutput, calls=%fused_computation.41 | convolution fusion | flops 406847488 | bytes 2363392 | tf_op jit(solution)/shard_map/bup,buv->bpv/dot_general | solution.py:57
  271.9 5.6 %convolution_subtract_fusion = f32[4,512,128]{2,1,0:T(8,128)S(1)} fusion(f32[4,512,128]{2,1,0:T(8,128)S(1)} %fusion.54, s32[512]{0:T(512)S(1)} %iota_add_fusion.2, s32[4,128]{1,0:T(4,128)S(1)} %get-tuple-element.12, f32[4,2,128,128]{3,2,0,1:T(8,128)S(1)} %all_gather.15), kind=kOutput, calls=%fused_computation.42 | convolution fusion | flops 406847488 | bytes 2363392 | tf_op jit(solution)/shard_map/bup,buv->bpv/dot_general | solution.py:54
  277.6 11.3 %fusion.26 = f32[512,1024,1]{1,0,2:T(8,128)S(1)} fusion(f32[4,512,128]{2,1,0:T(8,128)S(1)} %convolution_subtract_fusion, s32[1024]{0:T(1024)S(1)} %iota_add_fusion, s32[4,128]{1,0:T(4,128)S(1)} %get-tuple-element.11), kind=kOutput, calls=%fused_computation.45 | convolution fusion | flops 3229089792 | bytes 3151872 | tf_op jit(solution)/shard_map/bpv,bvq->pq/dot_general | solution.py:60
  288.9 11.9 %fusion.5 = f32[512,1024]{1,0:T(8,128)S(1)} fusion(f32[512,1024]{1,0:T(8,128)S(1)} %copy-done.2, f32[512,1024,1]{1,0,2:T(8,128)S(1)} %fusion.26, f32[64,8,8,128]{3,2,1,0:T(8,128)S(1)} %bitcast.165, f32[4,512,128]{2,1,0:T(8,128)S(1)} %convolution_add_fusion, s32[1024]{0:T(1024)S(1)} %iota_add_fusion, s32[4,128]{1,0:T(4,128)S(1)} %get-tuple-element.11), kind=kOutput, calls=%fused_computation.12 | convolution fusion | flops 3231711232 | bytes 9443328 | tf_op jit(solution)/shard_map/bpv,bvq->pq/dot_general | solution.py:60
  300.8 11.7 %fusion.9 = f32[4,128,512]{2,1,0:T(8,128)S(1)} fusion(s32[1024]{0:T(1024)S(1)} %iota_add_fusion, s32[4,128]{1,0:T(4,128)S(1)} %get-tuple-element.11, f32[512,1024]{1,0:T(8,128)S(1)} %copy-done.2, f32[512,1024]{1,0:T(8,128)S(1)} %fusion.5), kind=kOutput, calls=%fused_computation.16 | convolution fusion | flops 3230138368 | bytes 5249024 | tf_op jit(solution)/shard_map/pq,bvq->bpv/dot_general | solution.py:40
  312.5 11.5 %fusion.23 = f32[4,128,512]{2,1,0:T(8,128)S(1)} fusion(s32[1024]{0:T(1024)S(1)} %iota_add_fusion, s32[4,128]{1,0:T(4,128)S(1)} %get-tuple-element.11, f32[512,1024]{1,0:T(8,128)S(1)} %copy-done.2, f32[512,1024]{1,0:T(8,128)S(1)} %fusion.5), kind=kOutput, calls=%fused_computation.40 | convolution fusion | flops 3230400512 | bytes 5249024 | tf_op jit(solution)/shard_map/pq,bvq->bpv/dot_general | solution.py:41
  349.5 72.7 %lowrank.3 = f32[32,128,128]{2,1,0:T(8,128)S(1)} custom-call(f32[32,128,128]{2,1,0:T(8,128)S(1)} %bitcast.161, f32[1]{0:T(128)S(6)} %copy.49.radius_ref), custom_call_target="tpu_custom_call" | custom-call | tf_op jit(solution)/shard_map/lowrank/pallas_call | solution.py:232
  425.9 11.1 %psum.31 = f32[2]{0:T(128)S(1)} all-reduce(f32[2]{0:T(128)S(1)} %multiply_reduce_fusion), channel_id=1, replica_groups=mesh['chan'=32,'facet'=4,'vis'=2] {'facet'}, use_global_device_ids=true, to_apply=%region_5.6 | all-reduce | flops 2 | bytes 16 | tf_op jit(solution)/shard_map/psum | solution.py:288
  (54 shorter events, 62.8 us)
Async XLA Ops:
  7.2 205.4 %all-reduce.3.cloned.1.call-start = ((), (), s32[]{:S(2)}) async-start(), calls=%async_computation | async-start | bytes 1048576 | tf_op jit(solution)/shard_map/psum | solution.py:279
  59.0 11.4 %copy-start.3 = (f32[1,512,1024]{2,1,0:T(8,128)S(1)}, f32[1,512,1024]{2,1,0:T(8,128)}, u32[]{:S(2)}) copy-start(f32[1,512,1024]{2,1,0:T(8,128)} %param.8) | copy-start | bytes 6291460
  59.0 11.4 %copy-start.4 = (f32[1,512,1024]{2,1,0:T(8,128)S(1)}, f32[1,512,1024]{2,1,0:T(8,128)}, u32[]{:S(2)}) copy-start(f32[1,512,1024]{2,1,0:T(8,128)} %param.7) | copy-start | bytes 6291460
  82.3 44.6 %copy-start.1 = (f32[512,1024]{1,0:T(8,128)}, f32[512,1024]{1,0:T(8,128)S(1)}, u32[]{:S(2)}) copy-start(f32[512,1024]{1,0:T(8,128)S(1)} %fusion.19) | copy-start | bytes 6291460
  126.9 296.6 %all-reduce.5.cloned.1.call-start = ((), (), s32[]{:S(2)}) async-start(), calls=%async_computation.1 | async-start | bytes 1048576 | tf_op jit(solution)/shard_map/psum | solution.py:279
  131.3 81.3 %copy-start.6 = (f32[1,2,2,32,128]{4,3,2,1,0:T(8,128)S(1)}, f32[1,2,2,32,128]{4,3,2,1,0:T(8,128)}, u32[]{:S(2)}) copy-start(f32[1,2,2,32,128]{4,3,2,1,0:T(8,128)} %param.10) | copy-start | bytes 196612
  131.4 81.3 %copy-start.7 = (f32[1,2,2,32,128]{4,3,2,1,0:T(8,128)S(1)}, f32[1,2,2,32,128]{4,3,2,1,0:T(8,128)}, u32[]{:S(2)}) copy-start(f32[1,2,2,32,128]{4,3,2,1,0:T(8,128)} %param.9) | copy-start | bytes 196612
  211.3 1.3 copy-start
  213.6 13.3 %copy-start.8 = (f32[1,2]{1,0:T(1,128)S(1)}, f32[1,2]{1,0:T(1,128)}, u32[]{:S(2)}) copy-start(f32[1,2]{1,0:T(1,128)} %param.11) | copy-start | bytes 28
  277.6 11.3 %copy-start.2 = (f32[512,1024]{1,0:T(8,128)S(1)}, f32[512,1024]{1,0:T(8,128)}, u32[]{:S(2)}) copy-start(f32[512,1024]{1,0:T(8,128)} %copy-done.1) | copy-start | bytes 6291460
  300.8 11.7 %copy-start.5 = (f32[512,1024]{1,0:T(8,128)}, f32[512,1024]{1,0:T(8,128)S(1)}, u32[]{:S(2)}) copy-start(f32[512,1024]{1,0:T(8,128)S(1)} %fusion.5) | copy-start | bytes 6291460
Sparse Core Ops, SparseCore 0:
  127.0 77.4 all-reduce.2
  345.5 70.4 all-reduce.4

commit v2 on v1

v2 whole, which is shorter than its diff:
```python
import functools
import math

import jax
import jax.numpy as jnp
import numpy as np
from jax import lax
from jax.experimental import pallas as pl
from jax.experimental.pallas import tpu as pltpu
from jax.sharding import PartitionSpec as P

IMAGE = 2048
TILE = 128
BLOCKS = 4
NS_STEPS = 10
ITERS = 2
CHANNELS = 32
ROWS = 512
COLS = 1024
CHUNK = 256
PITCH = 136


step_size = 0.5
highest = lax.Precision.HIGHEST


def chan_peer(offset):
    me = lax.axis_index("chan")
    dy, dx, dc = offset
    y = lax.rem(me // 8 + dy, 4)
    x = lax.rem(me // 2 + dx, 4)
    return (y * 4 + x) * 2 + lax.rem(me + dc, 2)


def hops(offset):
    return min(offset[0], 4 - offset[0]) + min(offset[1], 4 - offset[1])


OFFSETS = sorted(
    [(dy, dx, dc) for dy in range(4) for dx in range(4) for dc in range(2) if (dy, dx, dc) != (0, 0, 0)],
    key=lambda offset: -hops(offset),
)
GROUP_A = [(0, dx, dc) for dx in (2, 1, 3, 0) for dc in range(2) if (dx, dc) != (0, 0)]
GROUP_B = [(dy, dv) for dv in (1, 0) for dy in (2, 1, 3, 0) if (dy, dv) != (0, 0)]


Z_OFFSETS = (4, 3, 5, 2, 6, 1, 7)


def group_b_device(offset):
    me = lax.axis_index("chan")
    return {
        "chan": lax.rem(me // 8 + offset[0], 4) * 8 + lax.rem(me, 8),
        "vis": lax.rem(lax.axis_index("vis") + offset[1], 2),
    }


def remote(source, target, send_sem, recv_sem, device):
    return pltpu.make_async_remote_copy(
        src_ref=source,
        dst_ref=target,
        send_sem=send_sem,
        recv_sem=recv_sem,
        device_id=device,
        device_id_type=pl.DeviceIdType.MESH,
    )


def split_bf16(value):
    high = value.astype(jnp.bfloat16)
    return high, (value - high.astype(jnp.float32)).astype(jnp.bfloat16)


def z_device(offset):
    z = lax.rem(lax.axis_index("vis") * 4 + lax.axis_index("facet") + offset, 8)
    return {"facet": lax.rem(z, 4), "vis": z // 4}


def facet_device(offset):
    return {"facet": lax.rem(lax.axis_index("facet") + offset, 4)}


def entry_barrier():
    barrier = pltpu.get_barrier_semaphore()
    peers = [{"chan": chan_peer(offset)} for offset in OFFSETS]
    peers += [group_b_device(offset) for offset in GROUP_B if offset[0] and offset[1]]
    peers += [z_device(offset) for offset in Z_OFFSETS]
    for device in peers:
        pl.semaphore_signal(barrier, inc=1, device_id=device, device_id_type=pl.DeviceIdType.MESH)
    pl.semaphore_wait(barrier, len(peers))


def sum_group(value, send_buf, recv_buf, sends, recvs, devices):
    send_buf[...] = value
    copies = []
    for n, device in enumerate(devices):
        copies.append(remote(send_buf, recv_buf.at[n], sends.at[n], recvs.at[n], device))
        copies[-1].start()
    for copy in copies:
        copy.wait()
    for n in range(len(devices)):
        value = value + recv_buf[n]
    return value


def stripes(group):
    return [pl.ds(group * 8 + s, CHANNELS, stride=PITCH) for s in range(8)]


def gram_of(received, halves):
    def body(group, total):
        block = jnp.concatenate([received[rows, :] for rows in stripes(group)], axis=1)
        both = jnp.concatenate(split_bf16(block), axis=0)
        halves[group] = both
        return total + lax.dot_general(
            both, both, (((1,), (1,)), ((), ())), preferred_element_type=jnp.float32
        )

    total = lax.fori_loop(0, TILE // 8, body, jnp.zeros((2 * CHANNELS, 2 * CHANNELS), jnp.float32))
    total = total[:CHANNELS] + total[CHANNELS:]
    return total[:, :CHANNELS] + total[:, CHANNELS:]


def mix_into(target, halves, root):
    high, low = split_bf16(root)
    weights = jnp.concatenate(
        [jnp.concatenate([high, high], axis=1), jnp.concatenate([low, low], axis=1)], axis=0
    )

    def body(group, carry):
        mixed = jnp.dot(weights, halves[group], preferred_element_type=jnp.float32)
        mixed = mixed[:CHANNELS] + mixed[CHANNELS:]
        for s, rows in enumerate(stripes(group)):
            target[rows, :] = mixed[:, s * 128 : (s + 1) * 128]
        return carry

    lax.fori_loop(0, TILE // 8, body, 0)


def matmul(a, b):
    return jnp.dot(a, b, precision=highest, preferred_element_type=jnp.float32)


def inverse_root(gram, radius):
    rows = lax.broadcasted_iota(jnp.int32, gram.shape, 0)
    eye = jnp.where(rows == lax.broadcasted_iota(jnp.int32, gram.shape, 1), 1.0, 0.0)
    matrix = eye + gram / (radius * radius)
    trace = jnp.sum(matrix * eye, axis=(0, 1), keepdims=True)
    current = matrix / trace
    inverse = eye
    for step in range(NS_STEPS):
        product = matmul(inverse, current) if step else current
        middle = 1.5 * eye - 0.5 * product
        inverse = matmul(middle, inverse) if step else middle
        if step < NS_STEPS - 1:
            current = matmul(current, middle)
    return inverse / jnp.sqrt(trace)


def pack(gram):
    return jnp.concatenate([gram[8 * k : 8 * k + 8] for k in range(4)], axis=1)


def unpack(packed):
    return jnp.concatenate([packed[:, 32 * k : 32 * k + 32] for k in range(4)], axis=0)


def lane_rows(index):
    return pl.ds(pl.multiple_of(index * PITCH, 8), TILE)


def waves():
    frequency = np.arange(TILE)
    angle = np.outer(frequency, np.arange(IMAGE)) % IMAGE * (2.0 * math.pi / IMAGE)
    table = np.stack([np.cos(angle), np.sin(angle)]) / math.sqrt(IMAGE)
    turn = np.outer(np.arange(16), np.arange(128)) % 16 * (2.0 * math.pi / 16)
    turns = np.stack([np.cos(turn), np.sin(turn)], axis=1)
    lanes = np.broadcast_to(turns[:, :, None, :], (16, 2, 8, 128))
    subs = np.broadcast_to(turns[:, :, :16, None], (16, 2, 16, 128))
    return [
        np.ascontiguousarray(value, dtype=np.float32)
        for value in (table, table.transpose(0, 2, 1), lanes, subs)
    ]


def turned(cosine, sine, turn, group):
    shape = cosine.shape
    cosine = cosine.reshape(shape[0] // group, group, shape[1])
    sine = sine.reshape(cosine.shape)
    c = cosine * turn[0] - sine * turn[1]
    s = sine * turn[0] + cosine * turn[1]
    return c.reshape(shape), s.reshape(shape)


def put(high_ref, low_ref, where, value):
    high, low = split_bf16(value)
    high_ref[where] = high
    low_ref[where] = low


def dot3(ah, al, bh, bl):
    def dot(a, b):
        return jnp.dot(a, b, preferred_element_type=jnp.float32)

    return dot(ah, bh) + dot(al, bh) + dot(ah, bl)


def build_tables(tiles_ref, wave_q, wave_p, waves_q, waves_p, lanes, subs, tabs):
    adj_h, adj_l, fwd_h, fwd_l, row_h, row_l, rowt_h, rowt_l = tabs

    def body(b, carry):
        turn_u = tiles_ref[b, 0]
        turn_v = tiles_ref[b, 1]
        lane_v = (lanes[turn_v, 0], lanes[turn_v, 1])
        lane_u = (lanes[turn_u, 0], lanes[turn_u, 1])
        sub_v = (subs[turn_v, 0], subs[turn_v, 1])
        sub_u = (subs[turn_u, 0], subs[turn_u, 1])
        first = pl.ds(pl.multiple_of(b * 256, 256), 128)
        second = pl.ds(pl.multiple_of(b * 256 + 128, 128), 128)
        for k in range(COLS // TILE):
            cols = slice(k * TILE, (k + 1) * TILE)
            half = slice(k % 2 * TILE, (k % 2 + 1) * TILE)
            c, s = turned(wave_q[0, :, cols], wave_q[1, :, cols], lane_v, 8)
            put(adj_h, adj_l, (k // 2, first, half), c)
            put(adj_h, adj_l, (k // 2, second, half), -s)
            c, s = turned(waves_q[0, cols], waves_q[1, cols], sub_v, 16)
            put(fwd_h, fwd_l, (b, cols, slice(0, 128)), c)
            put(fwd_h, fwd_l, (b, cols, slice(128, 256)), -s)
        for k in range(ROWS // TILE):
            cols = slice(k * TILE, (k + 1) * TILE)
            c, s = turned(wave_p[0, :, cols], wave_p[1, :, cols], lane_u, 8)
            put(row_h, row_l, (b, slice(0, 128), cols), c)
            put(row_h, row_l, (b, slice(128, 256), cols), s)
            c, s = turned(waves_p[0, cols], waves_p[1, cols], sub_u, 16)
            put(rowt_h, rowt_l, (b, cols, slice(0, 128)), c)
            put(rowt_h, rowt_l, (b, cols, slice(128, 256)), s)
        return carry

    lax.fori_loop(0, BLOCKS, body, 0)


def spread_rows(duals, rowt_h, rowt_l, e_h, e_l):
    def body(b, carry):
        side, block = b // 2, b % 2
        real = jnp.concatenate([duals[4 * side + f, block, 0] for f in range(4)], axis=0)
        imag = jnp.concatenate([duals[4 * side + f, block, 1] for f in range(4)], axis=0)
        both = jnp.concatenate(
            [jnp.concatenate([real, imag], axis=1), jnp.concatenate([-imag, real], axis=1)], axis=0
        )
        spread = dot3(rowt_h[b], rowt_l[b], *split_bf16(both))
        put(e_h, e_l, (slice(None), pl.ds(pl.multiple_of(b * 256, 256), 256)), spread)
        return carry

    lax.fori_loop(0, BLOCKS, body, 0)


def measure(x_h, x_l, tabs, values):
    adj_h, adj_l, fwd_h, fwd_l, row_h, row_l, rowt_h, rowt_l = tabs

    def body(b, carry):
        columns = dot3(x_h[...], x_l[...], fwd_h[b], fwd_l[b])
        quads = dot3(row_h[b], row_l[b], *split_bf16(columns))
        values[b, 0] = quads[:128, :128] + quads[128:, 128:]
        values[b, 1] = quads[:128, 128:] - quads[128:, :128]
        return carry

    lax.fori_loop(0, BLOCKS, body, 0)


def tile_place(j):
    rows = pl.ds(pl.multiple_of(j // 8 * TILE, TILE), TILE)
    cols = pl.ds(pl.multiple_of(lax.rem(j, 8) * TILE, TILE), TILE)
    return rows, cols


def negated(offset):
    return (-offset[0] % 4, -offset[1] % 4, -offset[2] % 2)


def imaging_kernel(
    x_hbm, p_hbm, dual_ref, data_ref, radii_ref, tiles_ref, radius_ref, wave_hbm, wavet_hbm, lanes, subs,
    x_out, p_out, dual_out,
    x_now, p_now, y_next, z_tiles, p_tiles, received, mixed, halves, x_h, x_l, e_h, e_l,
    adj_h, adj_l, fwd_h, fwd_l, row_h, row_l, rowt_h, rowt_l,
    wave_q, wave_p, waves_q, waves_p,
    duals, dual_mid, values, pieces, norm_send, norm_recv, sums, parts,
    local_sems, sends, recvs, z_sends, z_recvs, norm_sends, norm_recvs, small_sends, small_recvs,
):
    tabs = (adj_h, adj_l, fwd_h, fwd_l, row_h, row_l, rowt_h, rowt_l)
    me = lax.axis_index("chan")
    facet = lax.axis_index("facet")
    vis = lax.axis_index("vis")
    place = vis * 4 + facet
    at_q = pl.ds(pl.multiple_of(vis * COLS, COLS), COLS)
    at_p = pl.ds(pl.multiple_of(facet * ROWS, ROWS), ROWS)
    loads = [
        pltpu.make_async_copy(source, target, local_sems.at[n])
        for n, (source, target) in enumerate(
            [
                (wave_hbm.at[:, :, at_q], wave_q),
                (wave_hbm.at[:, :, at_p], wave_p),
                (wavet_hbm.at[:, at_q, :], waves_q),
                (wavet_hbm.at[:, at_p, :], waves_p),
                (x_hbm, x_now),
                (p_hbm, p_now),
            ]
        )
    ]
    for copy in loads:
        copy.start()
    entry_barrier()

    def gather_start(source, step):
        copies = []
        for n, offset in enumerate(Z_OFFSETS):
            copies.append(
                remote(source, duals.at[step, place], z_sends.at[step, n], z_recvs.at[step, n], z_device(offset))
            )
            copies[-1].start()
        return copies

    def column_chunk(d):
        return lax.rem(lax.rem(me // 2, 4) + d, 4)

    def adjoint_chunk(chunk):
        return dot3(e_h[...], e_l[...], adj_h[chunk], adj_l[chunk])

    index_of = {offset: n for n, offset in enumerate(OFFSETS)}

    def send_tile(step, source, target, offset):
        n = index_of[offset]
        copy = remote(source, target, sends.at[step, n], recvs.at[step, n], {"chan": chan_peer(offset)})
        copy.start()
        return copy

    def measure_and_update(step, dual_now, dual_next):
        measure(x_h, x_l, tabs, values)
        copies = []
        for n, offset in enumerate(Z_OFFSETS):
            device = z_device(offset)
            blocks = pl.ds(device["vis"] * 2, 2)
            rows = pl.ds(pl.multiple_of(device["facet"] * 32, 32), 32)
            copies.append(
                remote(values.at[blocks, :, rows, :], pieces.at[step, n], z_sends.at[2 + step, n],
                       z_recvs.at[2 + step, n], device)
            )
            copies[-1].start()
        for copy in copies:
            copy.wait()
        own = values[pl.ds(vis * 2, 2), :, pl.ds(pl.multiple_of(facet * 32, 32), 32), :]
        for n in range(len(Z_OFFSETS)):
            own = own + pieces[step, n]
        updated = dual_now[...] + own
        error = updated - data_ref[...]
        squares = jnp.sum((error * error).reshape(2, 8, 8, 128), axis=1)
        norm_send[step] = squares
        copies = []
        for n in range(3):
            copies.append(
                remote(norm_send.at[step], norm_recv.at[step, n], norm_sends.at[step, n], norm_recvs.at[step, n],
                       facet_device(n + 1))
            )
            copies[-1].start()
        for copy in copies:
            copy.wait()
        for n in range(3):
            squares = squares + norm_recv[step, n]
        for b in range(2):
            norm = jnp.sqrt(jnp.sum(squares[b], axis=(0, 1), keepdims=True))
            radius = radii_ref[b]
            factor = radius / jnp.maximum(norm, radius)
            dual_next[b] = updated[b] - (data_ref[b] + error[b] * factor)

    def gram_root(step):
        total = pack(gram_of(received.at[step], halves))
        total = sum_group(
            total, sums.at[2 * step], parts.at[2 * step], small_sends.at[2 * step], small_recvs.at[2 * step],
            [{"chan": chan_peer(offset)} for offset in GROUP_A],
        )
        return sum_group(
            total, sums.at[2 * step + 1], parts.at[2 * step + 1], small_sends.at[2 * step + 1],
            small_recvs.at[2 * step + 1], [group_b_device(offset) for offset in GROUP_B],
        )

    gathers = gather_start(dual_ref, 0)
    duals[0, place] = dual_ref[...]
    for copy in loads[:4]:
        copy.wait()
    build_tables(tiles_ref, wave_q, wave_p, waves_q, waves_p, lanes, subs, tabs)
    for copy in loads[4:]:
        copy.wait()
    for copy in gathers:
        copy.wait()
    spread_rows(duals.at[0], rowt_h, rowt_l, e_h, e_l)

    outward = []
    for d in (2, 1, 3, 0):
        chunk = column_chunk(d)
        gradient = adjoint_chunk(chunk)
        cols = pl.ds(pl.multiple_of(chunk * CHUNK, CHUNK), CHUNK)
        x = x_now[:, cols]
        p = p_now[:, cols]
        x_new = jnp.maximum(0.0, x - step_size * (p + gradient))
        bar = 2.0 * x_new - x
        x_now[:, cols] = x_new
        put(x_h, x_l, (slice(None), cols), bar)
        z = p + bar
        for i in range(4):
            for k in range(2):
                z_tiles[i * 8 + chunk * 2 + k] = z[i * TILE : (i + 1) * TILE, k * TILE : (k + 1) * TILE]
        for dy in (2, 1, 3, 0):
            for dc in range(2):
                offset = (dy, d, dc)
                if offset == (0, 0, 0):
                    received[0, lane_rows(me), :] = z_tiles[me]
                else:
                    outward.append(
                        send_tile(0, z_tiles.at[chan_peer(offset)], received.at[0, lane_rows(me), :], offset)
                    )

    measure_and_update(0, dual_ref, dual_mid)
    for copy in outward:
        copy.wait()
    total = gram_root(0)
    duals[1, place] = dual_mid[...]
    gathers = gather_start(dual_mid, 1)
    mix_into(mixed, halves, inverse_root(unpack(total), radius_ref[0]))
    backward = [
        send_tile(1, mixed.at[lane_rows(chan_peer(offset)), :], p_tiles.at[me], offset) for offset in OFFSETS
    ]
    p_tiles[me] = mixed[lane_rows(me), :]
    for copy in gathers:
        copy.wait()
    spread_rows(duals.at[1], rowt_h, rowt_l, e_h, e_l)

    def next_gradient(chunk, carry):
        cols = pl.ds(pl.multiple_of(chunk * CHUNK, CHUNK), CHUNK)
        y_next[:, cols] = x_now[:, cols] - step_size * adjoint_chunk(chunk)
        return carry

    lax.fori_loop(0, COLS // CHUNK, next_gradient, 0)

    outward = []
    for n, offset in enumerate(OFFSETS + [(0, 0, 0)]):
        away = negated(offset)
        j = chan_peer(away)
        if n < len(OFFSETS):
            backward[n].wait_recv()
        rows, cols = tile_place(j)
        x = x_now[rows, cols]
        p = p_tiles[j]
        x_new = jnp.maximum(0.0, y_next[rows, cols] - step_size * p)
        bar = 2.0 * x_new - x
        x_now[rows, cols] = x_new
        put(x_h, x_l, (rows, cols), bar)
        z = p + bar
        if n < len(OFFSETS):
            z_tiles[j] = z
            outward.append(send_tile(2, z_tiles.at[j], received.at[1, lane_rows(me), :], away))
        else:
            received[1, lane_rows(me), :] = z
    x_store = pltpu.make_async_copy(x_now, x_out, local_sems.at[6])
    x_store.start()
    measure_and_update(1, dual_mid, dual_out)
    for copy in backward:
        copy.wait_send()
    for copy in outward:
        copy.wait()
    total = gram_root(1)
    mix_into(mixed, halves, inverse_root(unpack(total), radius_ref[0]))
    rows, cols = tile_place(me)
    p_store = pltpu.make_async_copy(mixed.at[lane_rows(me), :], p_out.at[rows, cols], local_sems.at[7])
    p_store.start()
    backward = [
        send_tile(3, mixed.at[lane_rows(chan_peer(offset)), :], p_out.at[rows, cols], offset)
        for offset in OFFSETS
    ]
    x_store.wait()
    p_store.wait()
    for copy in backward:
        copy.wait()


def on_device(cube, lowrank_dual, vis_dual, visibilities, radii, tiles, facet_radius):
    f32, bf16 = jnp.float32, jnp.bfloat16
    dma = pltpu.SemaphoreType.DMA
    vmem = pl.BlockSpec(memory_space=pltpu.VMEM)
    smem = pl.BlockSpec(memory_space=pltpu.SMEM)
    anywhere = pl.BlockSpec(memory_space=pl.ANY)
    own = vis_dual.shape[1:]
    image = (ROWS, COLS)
    cube_next, lowrank_next, vis_next = pl.pallas_call(
        imaging_kernel,
        out_shape=[
            jax.ShapeDtypeStruct(image, f32),
            jax.ShapeDtypeStruct(image, f32),
            jax.ShapeDtypeStruct(own, f32),
        ],
        in_specs=[anywhere, anywhere, vmem, vmem, smem, smem, smem, anywhere, anywhere, vmem, vmem],
        out_specs=[anywhere, anywhere, vmem],
        scratch_shapes=[
            pltpu.VMEM(image, f32),
            pltpu.VMEM(image, f32),
            pltpu.VMEM(image, f32),
            pltpu.VMEM((CHANNELS, TILE, TILE), f32),
            pltpu.VMEM((CHANNELS, TILE, TILE), f32),
            pltpu.VMEM((2, CHANNELS * PITCH, TILE), f32),
            pltpu.VMEM((CHANNELS * PITCH, TILE), f32),
            pltpu.VMEM((TILE // 8, 2 * CHANNELS, 1024), bf16),
            pltpu.VMEM(image, bf16),
            pltpu.VMEM(image, bf16),
            pltpu.VMEM(image, bf16),
            pltpu.VMEM(image, bf16),
            pltpu.VMEM((COLS // CHUNK, BLOCKS * 256, CHUNK), bf16),
            pltpu.VMEM((COLS // CHUNK, BLOCKS * 256, CHUNK), bf16),
            pltpu.VMEM((BLOCKS, COLS, 256), bf16),
            pltpu.VMEM((BLOCKS, COLS, 256), bf16),
            pltpu.VMEM((BLOCKS, 256, ROWS), bf16),
            pltpu.VMEM((BLOCKS, 256, ROWS), bf16),
            pltpu.VMEM((BLOCKS, ROWS, 256), bf16),
            pltpu.VMEM((BLOCKS, ROWS, 256), bf16),
            pltpu.VMEM((2, TILE, COLS), f32),
            pltpu.VMEM((2, TILE, ROWS), f32),
            pltpu.VMEM((2, COLS, TILE), f32),
            pltpu.VMEM((2, ROWS, TILE), f32),
            pltpu.VMEM((2, 8) + own, f32),
            pltpu.VMEM(own, f32),
            pltpu.VMEM((BLOCKS, 2, TILE, TILE), f32),
            pltpu.VMEM((2, 7) + own, f32),
            pltpu.VMEM((2, 2, 8, 128), f32),
            pltpu.VMEM((2, 3, 2, 8, 128), f32),
            pltpu.VMEM((4, 8, 128), f32),
            pltpu.VMEM((4, 7, 8, 128), f32),
            dma((8,)),
            dma((4, 31)),
            dma((4, 31)),
            dma((4, 7)),
            dma((4, 7)),
            dma((2, 3)),
            dma((2, 3)),
            dma((4, 7)),
            dma((4, 7)),
        ],
        compiler_params=pltpu.CompilerParams(
            collective_id=0, has_side_effects=True, vmem_limit_bytes=56 << 20
        ),
        name="imaging",
    )(
        cube[0], lowrank_dual[0], vis_dual[0], visibilities[0], radii[0], tiles[0], facet_radius,
        *[jnp.asarray(value) for value in waves()],
    )
    return (cube_next[None], lowrank_next[None], vis_next[None])


def solution(mesh):
    placed = (
        P("chan", "facet", "vis"),
        P("chan", "facet", "vis"),
        P("chan", "vis", None, "facet", None),
        P("chan", "vis", None, "facet", None),
        P("chan", "vis"),
        P("chan", None, None),
        P("facet"),
    )
    return jax.shard_map(
        on_device,
        mesh=mesh,
        in_specs=placed,
        out_specs=(
            P("chan", "facet", "vis"),
            P("chan", "facet", "vis"),
            P("chan", "vis", None, "facet", None),
        ),
        check_vma=False,
    )
```

time: 455 us -> 186 us (0.41); the launches traced: 446 us -> 183 us
  matrix products: 179 us -> 0 us
  blocking collectives: 76.8 us -> 0 us
  Pallas kernels: 153 us -> 175 us
  between operations: 15.5 us -> 1.3 us
  other arithmetic: 12.5 us -> 0 us
    dot_general x24 -> x0, matrix products: 179 us -> none  [the longest x2 23.8 us: adjoint_blocks(): jnp.einsum('bpv,bvq->pq', eimag, sin_v, precision=highest)]
    all_gather x4 -> x0, blocking collectives: 55.2 us -> none  [the longest x2 29.7 us: on_device(): dual_rows = lax.all_gather(dual_now, 'facet', axis=2, tiled=True)]
    pallas_call x2 -> x1, Pallas kernels: 153 us -> 175 us  [on_device(): pl.pallas_call(imaging_kernel, out_shape=[jax.ShapeDtypeStruct(image, f32...]
    psum x2 -> x0, blocking collectives: 21.6 us -> none  [on_device(): norms = jnp.sqrt(lax.psum(squares, 'facet'))]
    unnamed x2 -> x0, other arithmetic: 6.12 us -> none
  transfers between devices with their start and end apart: 2 -> 0, of which waited for: 0 -> 0; matrix products, arithmetic and copies ran while one was open for 2% -> 0% of each run, Pallas kernels for 34% -> 0%
where the time goes in v2:
time: 186 us; the launch traced here: 183 us
  Pallas kernels  175 us (94%)
  local copies, waits for them, and re-layouts  6.6 us (4%)
    pallas_call x1, Pallas kernels, on_device(): pl.pallas_call(imaging_kernel, out_shape=[jax.ShapeDtypeStruct(image, f32...  175 us
    unnamed x7, local copies, waits for them, and re-layouts  5.26 us

profile of v2, /device:TPU:8, one launch (start us, length us, event | category | flops | bytes accessed | tf_op | source)
XLA Modules:
  0.0 182.8 jit_solution(18377750247697273005)
XLA Ops:
  1.3 1.3 copy.14.tiles_ref
  2.6 174.9 %imaging.1 = (f32[512,1024]{1,0:T(8,128)}, f32[512,1024]{1,0:T(8,128)}, f32[2,2,32,128]{3,2,1,0:T(8,128)}) custom-call(f32[512,1024]{1,0:T(8,128)} %bitcast.11, f32[512,1024]{1,0:T(8,128)} %bitcast.12, f32[2,2,32,128]{3,2,1,0:T(8,128)} %bitcast.14, f32[2,2,32,128]{3,2,1,0:T(8,128)} %bitcast.15, f32[2]{0:T(128)} %bitcast.17, s32[4,2]{1,0:T(4,128)} %copy.14.tiles_ref, ...), custom_call_target="tpu_custom_call" | custom-call | tf_op jit(solution)/shard_map/imaging/pallas_call | solution.py:493
  177.5 0.0 copy-start
  177.6 3.3 %copy.19 = f32[1,512,1024]{2,1,0:T(8,128)} copy(f32[1,512,1024]{2,1,0:T(8,128)} %bitcast.10) | data formatting | bytes 4194304
  180.9 0.0 copy-done
  180.9 0.0 copy-start.1
  180.9 1.3 copy.20
  182.2 0.0 copy-done.1
  182.2 0.6 copy.21
Async XLA Ops:
  177.5 3.3 %copy-start = (f32[512,1024]{1,0:T(8,128)S(1)}, f32[512,1024]{1,0:T(8,128)}, u32[]{:S(2)}) copy-start(f32[512,1024]{1,0:T(8,128)} %get-tuple-element.7) | copy-start | bytes 6291460
  180.9 1.3 copy-start.1

commit v3 on v2

--- a/solution.py
+++ b/solution.py
@@ -33,14 +33,14 @@
     return (y * 4 + x) * 2 + lax.rem(me + dc, 2)
 
 
-def hops(offset):
-    return min(offset[0], 4 - offset[0]) + min(offset[1], 4 - offset[1])
-
-
-OFFSETS = sorted(
-    [(dy, dx, dc) for dy in range(4) for dx in range(4) for dc in range(2) if (dy, dx, dc) != (0, 0, 0)],
-    key=lambda offset: -hops(offset),
-)
+OFFSETS = [
+    (3, 3, 1), (2, 3, 0), (2, 2, 0), (1, 3, 1), (3, 1, 1), (3, 2, 1),
+    (0, 1, 0), (2, 1, 1), (0, 1, 1), (0, 3, 1), (1, 1, 1), (3, 0, 1),
+    (2, 2, 1), (2, 0, 0), (0, 2, 1), (3, 3, 0), (1, 2, 1), (1, 0, 0),
+    (0, 0, 1), (0, 2, 0), (1, 0, 1), (2, 1, 0), (3, 0, 0), (2, 3, 1),
+    (0, 3, 0), (3, 2, 0), (1, 2, 0), (1, 1, 0), (3, 1, 0), (1, 3, 0),
+    (2, 0, 1),
+]
 GROUP_A = [(0, dx, dc) for dx in (2, 1, 3, 0) for dc in range(2) if (dx, dc) != (0, 0)]
 GROUP_B = [(dy, dv) for dv in (1, 0) for dy in (2, 1, 3, 0) if (dy, dv) != (0, 0)]
 
@@ -91,26 +91,13 @@
     pl.semaphore_wait(barrier, len(peers))
 
 
-def sum_group(value, send_buf, recv_buf, sends, recvs, devices):
-    send_buf[...] = value
-    copies = []
-    for n, device in enumerate(devices):
-        copies.append(remote(send_buf, recv_buf.at[n], sends.at[n], recvs.at[n], device))
-        copies[-1].start()
-    for copy in copies:
-        copy.wait()
-    for n in range(len(devices)):
-        value = value + recv_buf[n]
-    return value
-
-
 def stripes(group):
     return [pl.ds(group * 8 + s, CHANNELS, stride=PITCH) for s in range(8)]
 
 
-def gram_of(received, halves):
+def gram_of(stripe, halves):
     def body(group, total):
-        block = jnp.concatenate([received[rows, :] for rows in stripes(group)], axis=1)
+        block = jnp.concatenate([stripe(rows) for rows in stripes(group)], axis=1)
         both = jnp.concatenate(split_bf16(block), axis=0)
         halves[group] = both
         return total + lax.dot_general(
@@ -210,8 +197,8 @@
     adj_h, adj_l, fwd_h, fwd_l, row_h, row_l, rowt_h, rowt_l = tabs
 
     def body(b, carry):
-        turn_u = tiles_ref[b, 0]
-        turn_v = tiles_ref[b, 1]
+        turn_u = tiles_ref[0, 0, b]
+        turn_v = tiles_ref[0, 1, b]
         lane_v = (lanes[turn_v, 0], lanes[turn_v, 1])
         lane_u = (lanes[turn_u, 0], lanes[turn_u, 1])
         sub_v = (subs[turn_v, 0], subs[turn_v, 1])
@@ -281,7 +268,7 @@
 def imaging_kernel(
     x_hbm, p_hbm, dual_ref, data_ref, radii_ref, tiles_ref, radius_ref, wave_hbm, wavet_hbm, lanes, subs,
     x_out, p_out, dual_out,
-    x_now, p_now, y_next, z_tiles, p_tiles, received, mixed, halves, x_h, x_l, e_h, e_l,
+    x_now, p_now, change, slope, p_back, got_change, got_x, got_slope, mixed, halves, x_h, x_l, e_h, e_l,
     adj_h, adj_l, fwd_h, fwd_l, row_h, row_l, rowt_h, rowt_l,
     wave_q, wave_p, waves_q, waves_p,
     duals, dual_mid, values, pieces, norm_send, norm_recv, sums, parts,
@@ -298,12 +285,12 @@
         pltpu.make_async_copy(source, target, local_sems.at[n])
         for n, (source, target) in enumerate(
             [
+                (x_hbm, x_now),
+                (p_hbm, p_now),
                 (wave_hbm.at[:, :, at_q], wave_q),
                 (wave_hbm.at[:, :, at_p], wave_p),
                 (wavet_hbm.at[:, at_q, :], waves_q),
                 (wavet_hbm.at[:, at_p, :], waves_p),
-                (x_hbm, x_now),
-                (p_hbm, p_now),
             ]
         )
     ]
@@ -323,18 +310,34 @@
     def column_chunk(d):
         return lax.rem(lax.rem(me // 2, 4) + d, 4)
 
+    def chunk_columns(chunk):
+        return pl.ds(pl.multiple_of(chunk * CHUNK, CHUNK), CHUNK)
+
     def adjoint_chunk(chunk):
         return dot3(e_h[...], e_l[...], adj_h[chunk], adj_l[chunk])
 
     index_of = {offset: n for n, offset in enumerate(OFFSETS)}
 
-    def send_tile(step, source, target, offset):
+    def send(step, source, target, offset):
         n = index_of[offset]
         copy = remote(source, target, sends.at[step, n], recvs.at[step, n], {"chan": chan_peer(offset)})
         copy.start()
         return copy
 
-    def measure_and_update(step, dual_now, dual_next):
+    def send_tiles(step, image, target, offsets):
+        copies = []
+        for offset in offsets:
+            if offset == (0, 0, 0):
+                target[lane_rows(me), :] = image[tile_place(me)]
+            else:
+                source = image.at[tile_place(chan_peer(offset))]
+                copies.append(send(step, source, target.at[lane_rows(me), :], offset))
+        return copies
+
+    def send_back(step, target):
+        return [send(step, mixed.at[step - 3, lane_rows(chan_peer(offset)), :], target, offset) for offset in OFFSETS]
+
+    def scatter_start(step):
         measure(x_h, x_l, tabs, values)
         copies = []
         for n, offset in enumerate(Z_OFFSETS):
@@ -346,6 +349,9 @@
                        z_recvs.at[2 + step, n], device)
             )
             copies[-1].start()
+        return copies
+
+    def update_dual(step, copies, dual_now, dual_next):
         for copy in copies:
             copy.wait()
         own = values[pl.ds(vis * 2, 2), :, pl.ds(pl.multiple_of(facet * 32, 32), 32), :]
@@ -368,117 +374,127 @@
             squares = squares + norm_recv[step, n]
         for b in range(2):
             norm = jnp.sqrt(jnp.sum(squares[b], axis=(0, 1), keepdims=True))
-            radius = radii_ref[b]
+            radius = radii_ref[0, b]
             factor = radius / jnp.maximum(norm, radius)
             dual_next[b] = updated[b] - (data_ref[b] + error[b] * factor)
 
-    def gram_root(step):
-        total = pack(gram_of(received.at[step], halves))
-        total = sum_group(
-            total, sums.at[2 * step], parts.at[2 * step], small_sends.at[2 * step], small_recvs.at[2 * step],
-            [{"chan": chan_peer(offset)} for offset in GROUP_A],
-        )
-        return sum_group(
-            total, sums.at[2 * step + 1], parts.at[2 * step + 1], small_sends.at[2 * step + 1],
-            small_recvs.at[2 * step + 1], [group_b_device(offset) for offset in GROUP_B],
-        )
+    def sum_start(step, value, devices):
+        sums[step] = value
+        copies = []
+        for n, device in enumerate(devices):
+            copies.append(
+                remote(sums.at[step], parts.at[step, n], small_sends.at[step, n], small_recvs.at[step, n], device)
+            )
+            copies[-1].start()
+        return copies
+
+    def sum_end(step, copies):
+        for copy in copies:
+            copy.wait()
+        value = sums[step]
+        for n in range(len(copies)):
+            value = value + parts[step, n]
+        return value
+
+    group_a = [{"chan": chan_peer(offset)} for offset in GROUP_A]
+    group_b = [group_b_device(offset) for offset in GROUP_B]
 
     gathers = gather_start(dual_ref, 0)
     duals[0, place] = dual_ref[...]
-    for copy in loads[:4]:
+    for copy in loads[:2]:
+        copy.wait()
+
+    def subtract(k, carry):
+        rows = pl.ds(pl.multiple_of(k * 64, 64), 64)
+        change[rows, :] = p_now[rows, :] - x_now[rows, :]
+        return carry
+
+    lax.fori_loop(0, ROWS // 64, subtract, 0)
+    first = send_tiles(0, change, got_change, OFFSETS + [(0, 0, 0)])
+    for copy in loads[2:]:
         copy.wait()
     build_tables(tiles_ref, wave_q, wave_p, waves_q, waves_p, lanes, subs, tabs)
-    for copy in loads[4:]:
-        copy.wait()
     for copy in gathers:
         copy.wait()
     spread_rows(duals.at[0], rowt_h, rowt_l, e_h, e_l)
 
-    outward = []
     for d in (2, 1, 3, 0):
         chunk = column_chunk(d)
-        gradient = adjoint_chunk(chunk)
-        cols = pl.ds(pl.multiple_of(chunk * CHUNK, CHUNK), CHUNK)
+        cols = chunk_columns(chunk)
         x = x_now[:, cols]
-        p = p_now[:, cols]
-        x_new = jnp.maximum(0.0, x - step_size * (p + gradient))
-        bar = 2.0 * x_new - x
+        x_new = jnp.maximum(0.0, x - step_size * (p_now[:, cols] + adjoint_chunk(chunk)))
+        put(x_h, x_l, (slice(None), cols), 2.0 * x_new - x)
         x_now[:, cols] = x_new
-        put(x_h, x_l, (slice(None), cols), bar)
-        z = p + bar
-        for i in range(4):
-            for k in range(2):
-                z_tiles[i * 8 + chunk * 2 + k] = z[i * TILE : (i + 1) * TILE, k * TILE : (k + 1) * TILE]
-        for dy in (2, 1, 3, 0):
-            for dc in range(2):
-                offset = (dy, d, dc)
-                if offset == (0, 0, 0):
-                    received[0, lane_rows(me), :] = z_tiles[me]
-                else:
-                    outward.append(
-                        send_tile(0, z_tiles.at[chan_peer(offset)], received.at[0, lane_rows(me), :], offset)
-                    )
-
-    measure_and_update(0, dual_ref, dual_mid)
-    for copy in outward:
-        copy.wait()
-    total = gram_root(0)
+    first += send_tiles(1, x_now, got_x, OFFSETS + [(0, 0, 0)])
+
+    update_dual(0, scatter_start(0), dual_ref, dual_mid)
+    gathers = gather_start(dual_mid, 1)
     duals[1, place] = dual_mid[...]
-    gathers = gather_start(dual_mid, 1)
-    mix_into(mixed, halves, inverse_root(unpack(total), radius_ref[0]))
-    backward = [
-        send_tile(1, mixed.at[lane_rows(chan_peer(offset)), :], p_tiles.at[me], offset) for offset in OFFSETS
-    ]
-    p_tiles[me] = mixed[lane_rows(me), :]
+    for copy in first:
+        copy.wait()
+    total = pack(gram_of(lambda rows: got_change[rows, :] + 2.0 * got_x[rows, :], halves))
+    small = sum_start(0, total, group_a)
     for copy in gathers:
         copy.wait()
     spread_rows(duals.at[1], rowt_h, rowt_l, e_h, e_l)
-
-    def next_gradient(chunk, carry):
-        cols = pl.ds(pl.multiple_of(chunk * CHUNK, CHUNK), CHUNK)
-        y_next[:, cols] = x_now[:, cols] - step_size * adjoint_chunk(chunk)
-        return carry
-
-    lax.fori_loop(0, COLS // CHUNK, next_gradient, 0)
-
-    outward = []
+    for d in (2, 1, 3, 0):
+        chunk = column_chunk(d)
+        slope[:, chunk_columns(chunk)] = adjoint_chunk(chunk)
+        if d == 2:
+            small = sum_start(1, sum_end(0, small), group_b)
+    second = send_tiles(2, slope, got_slope, OFFSETS + [(0, 0, 0)])
+    total = sum_end(1, small)
+    mix_into(mixed.at[0], halves, inverse_root(unpack(total), radius_ref[0]))
+    third = send_back(3, p_back.at[me])
+    p_back[me] = mixed[0, lane_rows(me), :]
+    for copy in second:
+        copy.wait()
+    total = gram_of(
+        lambda rows: jnp.maximum(mixed[0, rows, :] - got_x[rows, :], got_x[rows, :] - got_slope[rows, :]), halves
+    )
+    total = sum_end(2, sum_start(2, pack(total), group_a))
+    total = sum_end(3, sum_start(3, total, group_b))
+    mix_into(mixed.at[1], halves, inverse_root(unpack(total), radius_ref[0]))
+    rows, cols = tile_place(me)
+    p_store = pltpu.make_async_copy(mixed.at[1, lane_rows(me), :], p_out.at[rows, cols], local_sems.at[7])
+    p_store.start()
+    fourth = send_back(4, p_out.at[rows, cols])
+
     for n, offset in enumerate(OFFSETS + [(0, 0, 0)]):
-        away = negated(offset)
-        j = chan_peer(away)
+        j = chan_peer(negated(offset))
         if n < len(OFFSETS):
-            backward[n].wait_recv()
+            third[n].wait_recv()
         rows, cols = tile_place(j)
         x = x_now[rows, cols]
-        p = p_tiles[j]
-        x_new = jnp.maximum(0.0, y_next[rows, cols] - step_size * p)
-        bar = 2.0 * x_new - x
+        x_new = jnp.maximum(0.0, x - step_size * (p_back[j] + slope[rows, cols]))
+        put(x_h, x_l, (rows, cols), 2.0 * x_new - x)
         x_now[rows, cols] = x_new
-        put(x_h, x_l, (rows, cols), bar)
-        z = p + bar
-        if n < len(OFFSETS):
-            z_tiles[j] = z
-            outward.append(send_tile(2, z_tiles.at[j], received.at[1, lane_rows(me), :], away))
-        else:
-            received[1, lane_rows(me), :] = z
     x_store = pltpu.make_async_copy(x_now, x_out, local_sems.at[6])
     x_store.start()
-    measure_and_update(1, dual_mid, dual_out)
-    for copy in backward:
+    update_dual(1, scatter_start(1), dual_mid, dual_out)
+    for copy in third:
         copy.wait_send()
-    for copy in outward:
-        copy.wait()
-    total = gram_root(1)
-    mix_into(mixed, halves, inverse_root(unpack(total), radius_ref[0]))
-    rows, cols = tile_place(me)
-    p_store = pltpu.make_async_copy(mixed.at[lane_rows(me), :], p_out.at[rows, cols], local_sems.at[7])
-    p_store.start()
-    backward = [
-        send_tile(3, mixed.at[lane_rows(chan_peer(offset)), :], p_out.at[rows, cols], offset)
-        for offset in OFFSETS
-    ]
     x_store.wait()
     p_store.wait()
-    for copy in backward:
+    for copy in fourth:
+        copy.wait()
+
+
+def store_kernel(x_in, p_in, dual_in, x_out, p_out, dual_out, x_buf, p_buf, dual_buf, load_sems, store_sems):
+    moves = []
+    for source, buffer, target in ((x_in, x_buf, x_out), (p_in, p_buf, p_out)):
+        for k in range(4):
+            rows = slice(k * 128, (k + 1) * 128)
+            moves.append((source.at[rows], buffer.at[rows], target.at[0, rows]))
+    moves.append((dual_in, dual_buf, dual_out.at[0]))
+    loads = [pltpu.make_async_copy(a, b, load_sems.at[n]) for n, (a, b, c) in enumerate(moves)]
+    stores = [pltpu.make_async_copy(b, c, store_sems.at[n]) for n, (a, b, c) in enumerate(moves)]
+    for copy in loads:
+        copy.start()
+    for load, store in zip(loads, stores):
+        load.wait()
+        store.start()
+    for copy in stores:
         copy.wait()
 
 
@@ -503,10 +519,12 @@
             pltpu.VMEM(image, f32),
             pltpu.VMEM(image, f32),
             pltpu.VMEM(image, f32),
+            pltpu.VMEM(image, f32),
             pltpu.VMEM((CHANNELS, TILE, TILE), f32),
-            pltpu.VMEM((CHANNELS, TILE, TILE), f32),
+            pltpu.VMEM((CHANNELS * PITCH, TILE), f32),
+            pltpu.VMEM((CHANNELS * PITCH, TILE), f32),
+            pltpu.VMEM((CHANNELS * PITCH, TILE), f32),
             pltpu.VMEM((2, CHANNELS * PITCH, TILE), f32),
-            pltpu.VMEM((CHANNELS * PITCH, TILE), f32),
             pltpu.VMEM((TILE // 8, 2 * CHANNELS, 1024), bf16),
             pltpu.VMEM(image, bf16),
             pltpu.VMEM(image, bf16),
@@ -533,8 +551,8 @@
             pltpu.VMEM((4, 8, 128), f32),
             pltpu.VMEM((4, 7, 8, 128), f32),
             dma((8,)),
-            dma((4, 31)),
-            dma((4, 31)),
+            dma((5, 31)),
+            dma((5, 31)),
             dma((4, 7)),
             dma((4, 7)),
             dma((2, 3)),
@@ -547,10 +565,22 @@
         ),
         name="imaging",
     )(
-        cube[0], lowrank_dual[0], vis_dual[0], visibilities[0], radii[0], tiles[0], facet_radius,
+        cube[0], lowrank_dual[0], vis_dual[0], visibilities[0], radii, jnp.swapaxes(tiles, 1, 2), facet_radius,
         *[jnp.asarray(value) for value in waves()],
     )
-    return (cube_next[None], lowrank_next[None], vis_next[None])
+    return pl.pallas_call(
+        store_kernel,
+        out_shape=[
+            jax.ShapeDtypeStruct((1,) + image, f32),
+            jax.ShapeDtypeStruct((1,) + image, f32),
+            jax.ShapeDtypeStruct((1,) + own, f32),
+        ],
+        in_specs=[anywhere] * 3,
+        out_specs=[anywhere] * 3,
+        scratch_shapes=[pltpu.VMEM(image, f32), pltpu.VMEM(image, f32), pltpu.VMEM(own, f32), dma((9,)), dma((9,))],
+        compiler_params=pltpu.CompilerParams(vmem_limit_bytes=56 << 20),
+        name="store",
+    )(cube_next, lowrank_next, vis_next)
 
 
 def solution(mesh):

time: 186 us -> 173 us (0.930)
  local copies, waits for them, and re-layouts: 6.6 us -> 0 us
  Pallas kernels: 175 us -> 169 us
    pallas_call x1, Pallas kernels: 175 us -> 165 us  [on_device(): pl.pallas_call(imaging_kernel, out_shape=[jax.ShapeDtypeStruct(image, f32...]
    unnamed x7 -> x0, local copies, waits for them, and re-layouts: 5.26 us -> none
    pallas_call x0 -> x1, Pallas kernels: none -> 3.61 us  [on_device(): pl.pallas_call(store_kernel, out_shape=[jax.ShapeDtypeStruct((1,) + image...]
where the time goes in v3:
time: 173 us; the launch traced here: 171 us
  Pallas kernels  169 us (98%)
    pallas_call x1, Pallas kernels, on_device(): pl.pallas_call(imaging_kernel, out_shape=[jax.ShapeDtypeStruct(image, f32...  165 us
    pallas_call x1, Pallas kernels, on_device(): pl.pallas_call(store_kernel, out_shape=[jax.ShapeDtypeStruct((1,) + image...  3.61 us

profile of v3, /device:TPU:8, one launch (start us, length us, event | category | flops | bytes accessed | tf_op | source)
XLA Modules:
  0.0 170.5 jit_solution(16094624257228381693)
XLA Ops:
  1.3 165.5 %imaging.1 = (f32[512,1024]{1,0:T(8,128)}, f32[512,1024]{1,0:T(8,128)}, f32[2,2,32,128]{3,2,1,0:T(8,128)}) custom-call(f32[512,1024]{1,0:T(8,128)} %bitcast.5, f32[512,1024]{1,0:T(8,128)} %bitcast.6, f32[2,2,32,128]{3,2,1,0:T(8,128)} %bitcast.7, f32[2,2,32,128]{3,2,1,0:T(8,128)} %bitcast.8, f32[1,2]{1,0:T(1,128)} %radii_ref.1, s32[1,2,4]{2,1,0:T(2,128)} %bitcast.9, ...), custom_call_target="tpu_custom_call" | custom-call | tf_op jit(solution)/shard_map/imaging/pallas_call | solution.py:509
  166.7 3.6 %store.1 = (f32[1,512,1024]{2,1,0:T(8,128)}, f32[1,512,1024]{2,1,0:T(8,128)}, f32[1,2,2,32,128]{4,3,2,1,0:T(8,128)}) custom-call(f32[512,1024]{1,0:T(8,128)} %get-tuple-element.6.x_in, f32[512,1024]{1,0:T(8,128)} %get-tuple-element.7.p_in, f32[2,2,32,128]{3,2,1,0:T(8,128)} %get-tuple-element.8.dual_in), custom_call_target="tpu_custom_call" | custom-call | tf_op jit(solution)/shard_map/store/pallas_call | solution.py:571

commit v4 on v3

--- a/solution.py
+++ b/solution.py
@@ -104,7 +104,9 @@
             both, both, (((1,), (1,)), ((), ())), preferred_element_type=jnp.float32
         )
 
-    total = lax.fori_loop(0, TILE // 8, body, jnp.zeros((2 * CHANNELS, 2 * CHANNELS), jnp.float32))
+    total = lax.fori_loop(
+        0, TILE // 8, body, jnp.zeros((2 * CHANNELS, 2 * CHANNELS), jnp.float32), unroll=4
+    )
     total = total[:CHANNELS] + total[CHANNELS:]
     return total[:, :CHANNELS] + total[:, CHANNELS:]
 
@@ -122,7 +124,7 @@
             target[rows, :] = mixed[:, s * 128 : (s + 1) * 128]
         return carry
 
-    lax.fori_loop(0, TILE // 8, body, 0)
+    lax.fori_loop(0, TILE // 8, body, 0, unroll=4)
 
 
 def matmul(a, b):
@@ -227,11 +229,14 @@
     lax.fori_loop(0, BLOCKS, body, 0)
 
 
-def spread_rows(duals, rowt_h, rowt_l, e_h, e_l):
+def spread_rows(duals, gain_of, rowt_h, rowt_l, e_h, e_l):
     def body(b, carry):
         side, block = b // 2, b % 2
         real = jnp.concatenate([duals[4 * side + f, block, 0] for f in range(4)], axis=0)
         imag = jnp.concatenate([duals[4 * side + f, block, 1] for f in range(4)], axis=0)
+        if gain_of is not None:
+            gain = gain_of(side, block, jnp.sum(real * real + imag * imag, axis=(0, 1), keepdims=True))
+            real, imag = real * gain, imag * gain
         both = jnp.concatenate(
             [jnp.concatenate([real, imag], axis=1), jnp.concatenate([-imag, real], axis=1)], axis=0
         )
@@ -242,22 +247,18 @@
     lax.fori_loop(0, BLOCKS, body, 0)
 
 
-def measure(x_h, x_l, tabs, values):
+def measure(b, x_h, x_l, tabs, values):
     adj_h, adj_l, fwd_h, fwd_l, row_h, row_l, rowt_h, rowt_l = tabs
-
-    def body(b, carry):
-        columns = dot3(x_h[...], x_l[...], fwd_h[b], fwd_l[b])
-        quads = dot3(row_h[b], row_l[b], *split_bf16(columns))
-        values[b, 0] = quads[:128, :128] + quads[128:, 128:]
-        values[b, 1] = quads[:128, 128:] - quads[128:, :128]
-        return carry
-
-    lax.fori_loop(0, BLOCKS, body, 0)
+    columns = dot3(x_h[...], x_l[...], fwd_h[b], fwd_l[b])
+    quads = dot3(row_h[b], row_l[b], *split_bf16(columns))
+    values[b, 0] = quads[:128, :128] + quads[128:, 128:]
+    values[b, 1] = quads[:128, 128:] - quads[128:, :128]
 
 
 def tile_place(j):
-    rows = pl.ds(pl.multiple_of(j // 8 * TILE, TILE), TILE)
-    cols = pl.ds(pl.multiple_of(lax.rem(j, 8) * TILE, TILE), TILE)
+    y, x, core = j // 8, lax.rem(j // 2, 4), lax.rem(j, 2)
+    rows = pl.ds(pl.multiple_of(y * TILE, TILE), TILE)
+    cols = pl.ds(pl.multiple_of((lax.rem(x + y, 4) * 2 + core) * TILE, TILE), TILE)
     return rows, cols
 
 
@@ -271,8 +272,9 @@
     x_now, p_now, change, slope, p_back, got_change, got_x, got_slope, mixed, halves, x_h, x_l, e_h, e_l,
     adj_h, adj_l, fwd_h, fwd_l, row_h, row_l, rowt_h, rowt_l,
     wave_q, wave_p, waves_q, waves_p,
-    duals, dual_mid, values, pieces, norm_send, norm_recv, sums, parts,
-    local_sems, sends, recvs, z_sends, z_recvs, norm_sends, norm_recvs, small_sends, small_recvs,
+    duals, error_mid, values, pieces, rad, gains, norm_send, norm_recv, sums, parts,
+    local_sems, sends, recvs, z_sends, z_recvs, scatter_sends, scatter_recvs, rad_sems,
+    norm_sends, norm_recvs, small_sends, small_recvs,
 ):
     tabs = (adj_h, adj_l, fwd_h, fwd_l, row_h, row_l, rowt_h, rowt_l)
     me = lax.axis_index("chan")
@@ -308,7 +310,7 @@
         return copies
 
     def column_chunk(d):
-        return lax.rem(lax.rem(me // 2, 4) + d, 4)
+        return lax.rem(lax.rem(me // 2, 4) + me // 8 + d, 4)
 
     def chunk_columns(chunk):
         return pl.ds(pl.multiple_of(chunk * CHUNK, CHUNK), CHUNK)
@@ -337,46 +339,63 @@
     def send_back(step, target):
         return [send(step, mixed.at[step - 3, lane_rows(chan_peer(offset)), :], target, offset) for offset in OFFSETS]
 
+    def chunk_offsets(d):
+        return [(dy, (d - dy) % 4, dc) for dc in range(2) for dy in (1, 3, 0, 2)]
+
     def scatter_start(step):
-        measure(x_h, x_l, tabs, values)
         copies = []
-        for n, offset in enumerate(Z_OFFSETS):
-            device = z_device(offset)
-            blocks = pl.ds(device["vis"] * 2, 2)
-            rows = pl.ds(pl.multiple_of(device["facet"] * 32, 32), 32)
-            copies.append(
-                remote(values.at[blocks, :, rows, :], pieces.at[step, n], z_sends.at[2 + step, n],
-                       z_recvs.at[2 + step, n], device)
-            )
-            copies[-1].start()
+        for away in (1, 0):
+            side = lax.rem(vis + away, 2)
+            for block in range(2):
+                measure(side * 2 + block, x_h, x_l, tabs, values)
+                for turn in (2, 1, 3, 0) if away else (2, 1, 3):
+                    owner = lax.rem(facet + turn, 4)
+                    rows = pl.ds(pl.multiple_of(owner * 32, 32), 32)
+                    n = turn + 3 if away else turn - 1
+                    copies.append(
+                        remote(values.at[side * 2 + block, :, rows, :], pieces.at[step, n, block],
+                               scatter_sends.at[step, n, block], scatter_recvs.at[step, n, block],
+                               {"facet": owner, "vis": side})
+                    )
+                    copies[-1].start()
         return copies
 
-    def update_dual(step, copies, dual_now, dual_next):
+    def residual(step, copies, dual_now):
         for copy in copies:
             copy.wait()
         own = values[pl.ds(vis * 2, 2), :, pl.ds(pl.multiple_of(facet * 32, 32), 32), :]
-        for n in range(len(Z_OFFSETS)):
+        for n in range(7):
             own = own + pieces[step, n]
-        updated = dual_now[...] + own
-        error = updated - data_ref[...]
+        return dual_now + own - data_ref[...]
+
+    def gain_of(side, block, squares):
+        radius = rad[side, block, 0:1, 0:1]
+        gain = 1.0 - radius / jnp.maximum(jnp.sqrt(squares), radius)
+        gains[side, block] = jnp.broadcast_to(gain, (8, 128))
+        return gain
+
+    def own_gain(block):
+        return gains[vis, block, 0:1, :]
+
+    def last_dual(copies):
+        now = jnp.stack([error_mid[b] * own_gain(b) for b in range(2)])
+        error = residual(1, copies, now)
         squares = jnp.sum((error * error).reshape(2, 8, 8, 128), axis=1)
-        norm_send[step] = squares
+        norm_send[...] = squares
         copies = []
         for n in range(3):
             copies.append(
-                remote(norm_send.at[step], norm_recv.at[step, n], norm_sends.at[step, n], norm_recvs.at[step, n],
-                       facet_device(n + 1))
+                remote(norm_send, norm_recv.at[n], norm_sends.at[n], norm_recvs.at[n], facet_device(n + 1))
             )
             copies[-1].start()
         for copy in copies:
             copy.wait()
         for n in range(3):
-            squares = squares + norm_recv[step, n]
+            squares = squares + norm_recv[n]
         for b in range(2):
             norm = jnp.sqrt(jnp.sum(squares[b], axis=(0, 1), keepdims=True))
             radius = radii_ref[0, b]
-            factor = radius / jnp.maximum(norm, radius)
-            dual_next[b] = updated[b] - (data_ref[b] + error[b] * factor)
+            dual_out[b] = error[b] - error[b] * (radius / jnp.maximum(norm, radius))
 
     def sum_start(step, value, devices):
         sums[step] = value
@@ -401,6 +420,10 @@
 
     gathers = gather_start(dual_ref, 0)
     duals[0, place] = dual_ref[...]
+    for b in range(2):
+        rad[vis, b] = jnp.full((8, 128), radii_ref[0, b], jnp.float32)
+    rad_copy = remote(rad.at[vis], rad.at[vis], rad_sems.at[0], rad_sems.at[1], {"vis": 1 - vis})
+    rad_copy.start()
     for copy in loads[:2]:
         copy.wait()
 
@@ -416,7 +439,7 @@
     build_tables(tiles_ref, wave_q, wave_p, waves_q, waves_p, lanes, subs, tabs)
     for copy in gathers:
         copy.wait()
-    spread_rows(duals.at[0], rowt_h, rowt_l, e_h, e_l)
+    spread_rows(duals.at[0], None, rowt_h, rowt_l, e_h, e_l)
 
     for d in (2, 1, 3, 0):
         chunk = column_chunk(d)
@@ -427,22 +450,22 @@
         x_now[:, cols] = x_new
     first += send_tiles(1, x_now, got_x, OFFSETS + [(0, 0, 0)])
 
-    update_dual(0, scatter_start(0), dual_ref, dual_mid)
-    gathers = gather_start(dual_mid, 1)
-    duals[1, place] = dual_mid[...]
-    for copy in first:
-        copy.wait()
-    total = pack(gram_of(lambda rows: got_change[rows, :] + 2.0 * got_x[rows, :], halves))
-    small = sum_start(0, total, group_a)
+    error_mid[...] = residual(0, scatter_start(0), dual_ref[...])
+    gathers = gather_start(error_mid, 1)
+    duals[1, place] = error_mid[...]
+    rad_copy.wait()
     for copy in gathers:
         copy.wait()
-    spread_rows(duals.at[1], rowt_h, rowt_l, e_h, e_l)
+    spread_rows(duals.at[1], gain_of, rowt_h, rowt_l, e_h, e_l)
+    second = []
     for d in (2, 1, 3, 0):
         chunk = column_chunk(d)
         slope[:, chunk_columns(chunk)] = adjoint_chunk(chunk)
-        if d == 2:
-            small = sum_start(1, sum_end(0, small), group_b)
-    second = send_tiles(2, slope, got_slope, OFFSETS + [(0, 0, 0)])
+        second += send_tiles(2, slope, got_slope, chunk_offsets(d))
+    for copy in first:
+        copy.wait()
+    total = pack(gram_of(lambda rows: got_change[rows, :] + 2.0 * got_x[rows, :], halves))
+    small = sum_start(1, sum_end(0, sum_start(0, total, group_a)), group_b)
     total = sum_end(1, small)
     mix_into(mixed.at[0], halves, inverse_root(unpack(total), radius_ref[0]))
     third = send_back(3, p_back.at[me])
@@ -471,7 +494,7 @@
         x_now[rows, cols] = x_new
     x_store = pltpu.make_async_copy(x_now, x_out, local_sems.at[6])
     x_store.start()
-    update_dual(1, scatter_start(1), dual_mid, dual_out)
+    last_dual(scatter_start(1))
     for copy in third:
         copy.wait_send()
     x_store.wait()
@@ -547,16 +570,21 @@
             pltpu.VMEM((BLOCKS, 2, TILE, TILE), f32),
             pltpu.VMEM((2, 7) + own, f32),
             pltpu.VMEM((2, 2, 8, 128), f32),
-            pltpu.VMEM((2, 3, 2, 8, 128), f32),
+            pltpu.VMEM((2, 2, 8, 128), f32),
+            pltpu.VMEM((2, 8, 128), f32),
+            pltpu.VMEM((3, 2, 8, 128), f32),
             pltpu.VMEM((4, 8, 128), f32),
             pltpu.VMEM((4, 7, 8, 128), f32),
             dma((8,)),
             dma((5, 31)),
             dma((5, 31)),
-            dma((4, 7)),
-            dma((4, 7)),
-            dma((2, 3)),
-            dma((2, 3)),
+            dma((2, 7)),
+            dma((2, 7)),
+            dma((2, 7, 2)),
+            dma((2, 7, 2)),
+            dma((2,)),
+            dma((3,)),
+            dma((3,)),
             dma((4, 7)),
             dma((4, 7)),
         ],

time: 173 us -> 173 us (level)
  no operation moved by 1% of the time
where the time goes in v4:
time: 173 us; the launch traced here: 171 us
  Pallas kernels  170 us (98%)
    pallas_call x1, Pallas kernels, on_device(): pl.pallas_call(imaging_kernel, out_shape=[jax.ShapeDtypeStruct(image, f32...  166 us
    pallas_call x1, Pallas kernels, on_device(): pl.pallas_call(store_kernel, out_shape=[jax.ShapeDtypeStruct((1,) + image...  3.61 us

profile of v4, /device:TPU:8, one launch (start us, length us, event | category | flops | bytes accessed | tf_op | source)
XLA Modules:
  0.0 171.1 jit_solution(5527912794198276844)
XLA Ops:
  1.3 166.1 %imaging.1 = (f32[512,1024]{1,0:T(8,128)}, f32[512,1024]{1,0:T(8,128)}, f32[2,2,32,128]{3,2,1,0:T(8,128)}) custom-call(f32[512,1024]{1,0:T(8,128)} %bitcast.5, f32[512,1024]{1,0:T(8,128)} %bitcast.6, f32[2,2,32,128]{3,2,1,0:T(8,128)} %bitcast.7, f32[2,2,32,128]{3,2,1,0:T(8,128)} %bitcast.8, f32[1,2]{1,0:T(1,128)} %radii_ref.1, s32[1,2,4]{2,1,0:T(2,128)} %bitcast.9, ...), custom_call_target="tpu_custom_call" | custom-call | tf_op jit(solution)/shard_map/imaging/pallas_call | solution.py:532
  167.3 3.6 %store.1 = (f32[1,512,1024]{2,1,0:T(8,128)}, f32[1,512,1024]{2,1,0:T(8,128)}, f32[1,2,2,32,128]{4,3,2,1,0:T(8,128)}) custom-call(f32[512,1024]{1,0:T(8,128)} %get-tuple-element.6.x_in, f32[512,1024]{1,0:T(8,128)} %get-tuple-element.7.p_in, f32[2,2,32,128]{3,2,1,0:T(8,128)} %get-tuple-element.8.dual_in), custom_call_target="tpu_custom_call" | custom-call | tf_op jit(solution)/shard_map/store/pallas_call | solution.py:599

commit v5 on v4

--- a/solution.py
+++ b/solution.py
@@ -336,11 +336,8 @@
                 copies.append(send(step, source, target.at[lane_rows(me), :], offset))
         return copies
 
-    def send_back(step, target):
-        return [send(step, mixed.at[step - 3, lane_rows(chan_peer(offset)), :], target, offset) for offset in OFFSETS]
-
-    def chunk_offsets(d):
-        return [(dy, (d - dy) % 4, dc) for dc in range(2) for dy in (1, 3, 0, 2)]
+    def send_back(step, target, offsets):
+        return [send(step, mixed.at[step - 3, lane_rows(chan_peer(offset)), :], target, offset) for offset in offsets]
 
     def scatter_start(step):
         copies = []
@@ -454,34 +451,41 @@
     gathers = gather_start(error_mid, 1)
     duals[1, place] = error_mid[...]
     rad_copy.wait()
+    for copy in first:
+        copy.wait()
+    total = pack(gram_of(lambda rows: got_change[rows, :] + 2.0 * got_x[rows, :], halves))
+    small = sum_start(0, total, group_a)
     for copy in gathers:
         copy.wait()
     spread_rows(duals.at[1], gain_of, rowt_h, rowt_l, e_h, e_l)
-    second = []
-    for d in (2, 1, 3, 0):
-        chunk = column_chunk(d)
+    small = sum_start(1, sum_end(0, small), group_b)
+
+    def next_gradient(chunk, carry):
         slope[:, chunk_columns(chunk)] = adjoint_chunk(chunk)
-        second += send_tiles(2, slope, got_slope, chunk_offsets(d))
-    for copy in first:
-        copy.wait()
-    total = pack(gram_of(lambda rows: got_change[rows, :] + 2.0 * got_x[rows, :], halves))
-    small = sum_start(1, sum_end(0, sum_start(0, total, group_a)), group_b)
+        return carry
+
+    lax.fori_loop(0, COLS // CHUNK, next_gradient, 0)
     total = sum_end(1, small)
+    second = send_tiles(2, slope, got_slope, OFFSETS + [(0, 0, 0)])
     mix_into(mixed.at[0], halves, inverse_root(unpack(total), radius_ref[0]))
-    third = send_back(3, p_back.at[me])
+    third = send_back(3, p_back.at[me], OFFSETS[:8])
     p_back[me] = mixed[0, lane_rows(me), :]
     for copy in second:
         copy.wait()
     total = gram_of(
         lambda rows: jnp.maximum(mixed[0, rows, :] - got_x[rows, :], got_x[rows, :] - got_slope[rows, :]), halves
     )
-    total = sum_end(2, sum_start(2, pack(total), group_a))
-    total = sum_end(3, sum_start(3, total, group_b))
+    small = sum_start(2, pack(total), group_a)
+    third += send_back(3, p_back.at[me], OFFSETS[8:14])
+    small = sum_start(3, sum_end(2, small), group_b)
+    third += send_back(3, p_back.at[me], OFFSETS[14:20])
+    total = sum_end(3, small)
+    third += send_back(3, p_back.at[me], OFFSETS[20:])
     mix_into(mixed.at[1], halves, inverse_root(unpack(total), radius_ref[0]))
     rows, cols = tile_place(me)
     p_store = pltpu.make_async_copy(mixed.at[1, lane_rows(me), :], p_out.at[rows, cols], local_sems.at[7])
     p_store.start()
-    fourth = send_back(4, p_out.at[rows, cols])
+    fourth = send_back(4, p_out.at[rows, cols], OFFSETS)
 
     for n, offset in enumerate(OFFSETS + [(0, 0, 0)]):
         j = chan_peer(negated(offset))

time: 173 us -> 164 us (0.948)
  Pallas kernels: 170 us -> 162 us
    pallas_call x1, Pallas kernels: 166 us -> 159 us  [on_device(): pl.pallas_call(imaging_kernel, out_shape=[jax.ShapeDtypeStruct(image, f32...]
where the time goes in v5:
time: 164 us
  Pallas kernels  162 us (99%)
    pallas_call x1, Pallas kernels, on_device(): pl.pallas_call(imaging_kernel, out_shape=[jax.ShapeDtypeStruct(image, f32...  159 us
    pallas_call x1, Pallas kernels, on_device(): pl.pallas_call(store_kernel, out_shape=[jax.ShapeDtypeStruct((1,) + image...  3.61 us

profile of v5, /device:TPU:8, one launch (start us, length us, event | category | flops | bytes accessed | tf_op | source)
XLA Modules:
  0.0 163.8 jit_solution(4747268243315983827)
XLA Ops:
  1.3 158.7 %imaging.1 = (f32[512,1024]{1,0:T(8,128)}, f32[512,1024]{1,0:T(8,128)}, f32[2,2,32,128]{3,2,1,0:T(8,128)}) custom-call(f32[512,1024]{1,0:T(8,128)} %bitcast.5, f32[512,1024]{1,0:T(8,128)} %bitcast.6, f32[2,2,32,128]{3,2,1,0:T(8,128)} %bitcast.7, f32[2,2,32,128]{3,2,1,0:T(8,128)} %bitcast.8, f32[1,2]{1,0:T(1,128)} %radii_ref.1, s32[1,2,4]{2,1,0:T(2,128)} %bitcast.9, ...), custom_call_target="tpu_custom_call" | custom-call | tf_op jit(solution)/shard_map/imaging/pallas_call | solution.py:536
  160.0 3.6 %store.1 = (f32[1,512,1024]{2,1,0:T(8,128)}, f32[1,512,1024]{2,1,0:T(8,128)}, f32[1,2,2,32,128]{4,3,2,1,0:T(8,128)}) custom-call(f32[512,1024]{1,0:T(8,128)} %get-tuple-element.6.x_in, f32[512,1024]{1,0:T(8,128)} %get-tuple-element.7.p_in, f32[2,2,32,128]{3,2,1,0:T(8,128)} %get-tuple-element.8.dual_in), custom_call_target="tpu_custom_call" | custom-call | tf_op jit(solution)/shard_map/store/pallas_call | solution.py:603

commit v6 on v5

--- a/solution.py
+++ b/solution.py
@@ -339,6 +339,9 @@
     def send_back(step, target, offsets):
         return [send(step, mixed.at[step - 3, lane_rows(chan_peer(offset)), :], target, offset) for offset in offsets]
 
+    def chunk_offsets(d):
+        return [(dy, (d - dy) % 4, dc) for dc in range(2) for dy in (1, 3, 0, 2)]
+
     def scatter_start(step):
         copies = []
         for away in (1, 0):
@@ -459,14 +462,12 @@
         copy.wait()
     spread_rows(duals.at[1], gain_of, rowt_h, rowt_l, e_h, e_l)
     small = sum_start(1, sum_end(0, small), group_b)
-
-    def next_gradient(chunk, carry):
+    second = []
+    for d in (2, 1, 3, 0):
+        chunk = column_chunk(d)
         slope[:, chunk_columns(chunk)] = adjoint_chunk(chunk)
-        return carry
-
-    lax.fori_loop(0, COLS // CHUNK, next_gradient, 0)
+        second += send_tiles(2, slope, got_slope, chunk_offsets(d))
     total = sum_end(1, small)
-    second = send_tiles(2, slope, got_slope, OFFSETS + [(0, 0, 0)])
     mix_into(mixed.at[0], halves, inverse_root(unpack(total), radius_ref[0]))
     third = send_back(3, p_back.at[me], OFFSETS[:8])
     p_back[me] = mixed[0, lane_rows(me), :]

time: 164 us -> 165 us (level)
  no operation moved by 1% of the time
where the time goes in v6:
time: 165 us; the launch traced here: 163 us
  Pallas kernels  162 us (98%)
    pallas_call x1, Pallas kernels, on_device(): pl.pallas_call(imaging_kernel, out_shape=[jax.ShapeDtypeStruct(image, f32...  158 us
    pallas_call x1, Pallas kernels, on_device(): pl.pallas_call(store_kernel, out_shape=[jax.ShapeDtypeStruct((1,) + image...  3.61 us

profile of v6, /device:TPU:8, one launch (start us, length us, event | category | flops | bytes accessed | tf_op | source)
XLA Modules:
  0.0 163.1 jit_solution(6063735817650208865)
XLA Ops:
  1.3 158.1 %imaging.1 = (f32[512,1024]{1,0:T(8,128)}, f32[512,1024]{1,0:T(8,128)}, f32[2,2,32,128]{3,2,1,0:T(8,128)}) custom-call(f32[512,1024]{1,0:T(8,128)} %bitcast.5, f32[512,1024]{1,0:T(8,128)} %bitcast.6, f32[2,2,32,128]{3,2,1,0:T(8,128)} %bitcast.7, f32[2,2,32,128]{3,2,1,0:T(8,128)} %bitcast.8, f32[1,2]{1,0:T(1,128)} %radii_ref.1, s32[1,2,4]{2,1,0:T(2,128)} %bitcast.9, ...), custom_call_target="tpu_custom_call" | custom-call | tf_op jit(solution)/shard_map/imaging/pallas_call | solution.py:537
  159.4 3.6 %store.1 = (f32[1,512,1024]{2,1,0:T(8,128)}, f32[1,512,1024]{2,1,0:T(8,128)}, f32[1,2,2,32,128]{4,3,2,1,0:T(8,128)}) custom-call(f32[512,1024]{1,0:T(8,128)} %get-tuple-element.6.x_in, f32[512,1024]{1,0:T(8,128)} %get-tuple-element.7.p_in, f32[2,2,32,128]{3,2,1,0:T(8,128)} %get-tuple-element.8.dual_in), custom_call_target="tpu_custom_call" | custom-call | tf_op jit(solution)/shard_map/store/pallas_call | solution.py:604
